TPU v7x, 256 devices: a whole 4x4x8 slice. The times are simulated.
256 devices in a mesh: dp: 16 (over z_hi, y, core), ctx: 16 (over x, z_lo).
Axes of the slice: x: 4, y: 4, z: 8 (z_hi: 2, z_lo: 4; z = z_hi * 4 + z_lo), core: 2. Of those that a mesh axis runs over, the one named last changes fastest.
Arguments:
- query_nope: bfloat16 [16, 2048, 2048], P('dp', 'ctx'), may hold values from -6 to 6
- query_rope: bfloat16 [16, 2048, 1024], P('dp', 'ctx'), may hold values from -9 to 9
- latent: bfloat16 [16, 2048, 512], P('dp', 'ctx'), may hold values from -6 to 6
- key_rope: bfloat16 [16, 2048, 64], P('dp', 'ctx'), may hold values from -6 to 6
- grad_output: bfloat16 [16, 2048, 2048], P('dp', 'ctx'), may hold values from -6 to 6
- kv_up: bfloat16 [512, 4096], replicated, may hold values from -0.25 to 0.25
- doc_lengths: int32 [16, 8], P('dp'), may hold values from 1 to 1536, 2048 in all within a row
Outputs:
- grad_query_nope: bfloat16 [16, 2048, 2048], P('dp', 'ctx')
- grad_query_rope: bfloat16 [16, 2048, 1024], P('dp', 'ctx')
- grad_latent: bfloat16 [16, 2048, 512], P('dp', 'ctx')
- grad_key_rope: bfloat16 [16, 2048, 64], P('dp', 'ctx')
- grad_kv_up: float32 [512, 4096], P('ctx')
All inputs are finite; a program needn't handle non-finite values.
Results may differ from a plain program's by a relative error of at most 0.015.
Values may be sent and summed in bfloat16 or wider, within the bound.
A program may use at most 128 MiB of HBM per device.

v0:
```python
import jax
import jax.numpy as jnp
from jax import lax
from jax.sharding import PartitionSpec as P

HEAD_COUNT = 16
HEAD_DIM = 128
VALUE_DIM = 128
ROPE_DIM = 64
LATENT = 512


NEGATIVE = -1e30


def product(form, left, right):
    return jnp.einsum(form, left, right, preferred_element_type=jnp.float32)


def doc_bounds(lengths, positions):
    doc_ends = jnp.cumsum(lengths)
    before = doc_ends[None, :] <= positions[:, None]
    doc_ident = jnp.sum(before.astype(jnp.int32), axis=1)
    doc_first = jnp.max(jnp.where(before, doc_ends[None, :], 0), axis=1)
    return (doc_ident, doc_first)


def visible_block(query_pos, query_doc, key_first, extent, lengths):
    key_pos = key_first + jnp.arange(extent, dtype=jnp.int32)
    key_doc, unused_first = doc_bounds(lengths, key_pos)
    return (key_pos[None, :] <= query_pos[:, None]) & (key_doc[None, :] == query_doc[:, None])


def score_block(query_latent, query_rot, key_lat, key_rot, softmax_scale):
    direct = product("ihr,jr->hij", query_latent, key_lat)
    rotary = product("ihr,jr->hij", query_rot, key_rot)
    return softmax_scale * (direct + rotary)


def stats_update(state, scores, visible, grad_prob):
    row_max, row_sum, row_dot = state
    masked = jnp.where(visible[None], scores, NEGATIVE)
    new_max = jnp.maximum(row_max, jnp.max(masked, axis=2))
    attend = jnp.where(visible[None], jnp.exp(scores - new_max[:, :, None]), 0.0)
    factor = jnp.exp(row_max - new_max)
    return (
        new_max,
        row_sum * factor + jnp.sum(attend, axis=2),
        row_dot * factor + jnp.sum(attend * grad_prob, axis=2),
    )


def grad_update(
    state,
    scores,
    visible,
    grad_prob,
    log_total,
    inner_mean,
    key_lat,
    key_rot,
    query_latent,
    query_rot,
    output_grad,
    key_first,
    softmax_scale,
):
    acc_query, acc_rot, acc_out, acc_keys, acc_keyrot = state
    attend = jnp.where(visible[None], jnp.exp(scores - log_total[:, :, None]), 0.0)
    attend_low = attend.astype(jnp.bfloat16)
    grad_score = (attend * (grad_prob - inner_mean[:, :, None])).astype(jnp.bfloat16)
    acc_query = acc_query + product("hij,jr->ihr", grad_score, key_lat)
    acc_rot = acc_rot + product("hij,jr->ihr", grad_score, key_rot)
    acc_out = acc_out + product("hij,jr->ihr", attend_low, key_lat)
    key_part = softmax_scale * product("hij,ihr->jr", grad_score, query_latent) + product(
        "hij,ihr->jr", attend_low, output_grad
    )
    rot_part = softmax_scale * product("hij,ihr->jr", grad_score, query_rot)
    extent = key_lat.shape[0]
    acc_keys = lax.dynamic_update_slice_in_dim(
        acc_keys, lax.dynamic_slice_in_dim(acc_keys, key_first, extent, 0) + key_part, key_first, 0
    )
    acc_keyrot = lax.dynamic_update_slice_in_dim(
        acc_keyrot,
        lax.dynamic_slice_in_dim(acc_keyrot, key_first, extent, 0) + rot_part,
        key_first,
        0,
    )
    return (acc_query, acc_rot, acc_out, acc_keys, acc_keyrot)


def body(query_nope, query_rope, latent, key_rope, grad_output, kv_up, doc_lengths):
    tokens = query_nope.shape[1]
    devices = lax.axis_size("ctx")
    seq_total = tokens * devices
    lengths = doc_lengths[0]
    softmax_scale = (HEAD_DIM + ROPE_DIM) ** (-0.5)
    weights = kv_up.reshape(LATENT, HEAD_COUNT, HEAD_DIM + VALUE_DIM)
    key_weight = weights[:, :, :HEAD_DIM]
    value_weight = weights[:, :, HEAD_DIM:]
    nope_rows = query_nope[0].reshape(tokens, HEAD_COUNT, HEAD_DIM)
    rope_rows = query_rope[0].reshape(tokens, HEAD_COUNT, ROPE_DIM)
    grad_rows = grad_output[0].reshape(tokens, HEAD_COUNT, VALUE_DIM)
    query_latent = product("ihd,rhd->ihr", nope_rows, key_weight).astype(jnp.bfloat16)
    output_grad = product("ihe,rhe->ihr", grad_rows, value_weight).astype(jnp.bfloat16)
    query_pos = lax.axis_index("ctx") * tokens + jnp.arange(tokens, dtype=jnp.int32)
    query_doc, query_start = doc_bounds(lengths, query_pos)
    query_last = query_pos[tokens - 1]
    query_floor = query_start[0]

    def skipped(key_first, extent):
        return (key_first > query_last) | (key_first + extent - 1 < query_floor)

    def stats_step(state, key_lat, key_rot, key_first):
        extent = key_lat.shape[0]

        def stats_work(inner_state):
            scores = score_block(query_latent, rope_rows, key_lat, key_rot, softmax_scale)
            visible = visible_block(query_pos, query_doc, key_first, extent, lengths)
            grad_prob = product("ihr,jr->hij", output_grad, key_lat)
            return stats_update(inner_state, scores, visible, grad_prob)

        return lax.cond(
            skipped(key_first, extent), lambda inner_state: inner_state, stats_work, state
        )

    def make_grad_step(log_total, inner_mean):

        def grad_step(state, key_lat, key_rot, key_first):
            extent = key_lat.shape[0]

            def grad_work(inner_state):
                scores = score_block(query_latent, rope_rows, key_lat, key_rot, softmax_scale)
                visible = visible_block(query_pos, query_doc, key_first, extent, lengths)
                grad_prob = product("ihr,jr->hij", output_grad, key_lat)
                return grad_update(
                    inner_state,
                    scores,
                    visible,
                    grad_prob,
                    log_total,
                    inner_mean,
                    key_lat,
                    key_rot,
                    query_latent,
                    rope_rows,
                    output_grad,
                    key_first,
                    softmax_scale,
                )

            return lax.cond(
                skipped(key_first, extent), lambda inner_state: inner_state, grad_work, state
            )

        return grad_step

    first_state = (
        jnp.full((HEAD_COUNT, tokens), NEGATIVE, jnp.float32),
        jnp.zeros((HEAD_COUNT, tokens), jnp.float32),
        jnp.zeros((HEAD_COUNT, tokens), jnp.float32),
    )
    grad_state = (
        jnp.zeros((tokens, HEAD_COUNT, LATENT), jnp.float32),
        jnp.zeros((tokens, HEAD_COUNT, ROPE_DIM), jnp.float32),
        jnp.zeros((tokens, HEAD_COUNT, LATENT), jnp.float32),
        jnp.zeros((seq_total, LATENT), jnp.float32),
        jnp.zeros((seq_total, ROPE_DIM), jnp.float32),
    )
    all_latent, all_rot = (
        lax.all_gather(latent[0], "ctx", axis=0, tiled=True),
        lax.all_gather(key_rope[0], "ctx", axis=0, tiled=True),
    )
    key_block = min(512, seq_total)

    def stats_loop(index, state):
        key_first = (index * key_block).astype(jnp.int32)
        key_lat = lax.dynamic_slice_in_dim(all_latent, key_first, key_block, 0)
        key_rot = lax.dynamic_slice_in_dim(all_rot, key_first, key_block, 0)
        return stats_step(state, key_lat, key_rot, key_first)

    row_max, row_sum, row_dot = lax.fori_loop(0, seq_total // key_block, stats_loop, first_state)
    log_total = row_max + jnp.log(row_sum)
    inner_mean = row_dot / row_sum
    grad_step = make_grad_step(log_total, inner_mean)

    def grad_loop(index, state):
        key_first = (index * key_block).astype(jnp.int32)
        key_lat = lax.dynamic_slice_in_dim(all_latent, key_first, key_block, 0)
        key_rot = lax.dynamic_slice_in_dim(all_rot, key_first, key_block, 0)
        return grad_step(state, key_lat, key_rot, key_first)

    acc_query, acc_rot, acc_out, acc_keys, acc_keyrot = lax.fori_loop(
        0, seq_total // key_block, grad_loop, grad_state
    )
    owned_keys, owned_keyrot = (
        lax.psum_scatter(acc_keys, "ctx", scatter_dimension=0, tiled=True),
        lax.psum_scatter(acc_keyrot, "ctx", scatter_dimension=0, tiled=True),
    )
    query_latent_grad = (softmax_scale * acc_query).astype(jnp.bfloat16)
    grad_query_rope = (
        (softmax_scale * acc_rot).astype(jnp.bfloat16).reshape(tokens, HEAD_COUNT * ROPE_DIM)
    )
    out_latent = acc_out.astype(jnp.bfloat16)
    grad_query_nope = (
        product("ihr,rhd->ihd", query_latent_grad, key_weight)
        .astype(jnp.bfloat16)
        .reshape(tokens, HEAD_COUNT * HEAD_DIM)
    )
    rows_owned = LATENT // devices
    joined = jnp.concatenate(
        [
            product("ihr,ihd->rhd", query_latent_grad, nope_rows),
            product("ihr,ihe->rhe", out_latent, grad_rows),
        ],
        axis=2,
    )
    summed = lax.psum(joined.reshape(LATENT, HEAD_COUNT * (HEAD_DIM + VALUE_DIM)), ("dp", "ctx"))
    grad_kv_up = lax.dynamic_slice_in_dim(summed, lax.axis_index("ctx") * rows_owned, rows_owned, 0)
    return (
        grad_query_nope[None],
        grad_query_rope[None],
        owned_keys.astype(jnp.bfloat16)[None],
        owned_keyrot.astype(jnp.bfloat16)[None],
        grad_kv_up,
    )


def solution(mesh):
    return jax.shard_map(
        body,
        mesh=mesh,
        in_specs=(
            P("dp", "ctx", None),
            P("dp", "ctx", None),
            P("dp", "ctx", None),
            P("dp", "ctx", None),
            P("dp", "ctx", None),
            P(),
            P("dp", None),
        ),
        out_specs=(
            P("dp", "ctx", None),
            P("dp", "ctx", None),
            P("dp", "ctx", None),
            P("dp", "ctx", None),
            P("ctx", None),
        ),
        check_vma=False,
    )
```

profile of v0, /device:TPU:1, one launch (start us, length us, event | category | flops | bytes accessed | tf_op | source)
XLA Modules:
  0.0 699.0 jit_solution(2279497304872502732)
XLA Ops:
  7.2 0.7 all-gather.4.cloned.1.call-update
  8.0 0.6 slice.12
  8.5 0.8 reduce-window.28
  9.4 1.1 copy.56
  10.5 1.3 copy.76
  11.8 1.5 copy.77
  13.3 6.7 copy.53
  20.1 3.7 convert_bitcast_fusion.1
  23.8 2.9 copy.61
  26.7 3.7 convert_bitcast_fusion
  30.4 3.9 copy.60
  34.3 0.1 fusion.64
  34.4 42.5 %all-gather.1 = bf16[1,2048,64]{1,2,0:T(8,128)(2,1)S(1)} all-gather(bf16[1,128,64]{1,2,0:T(8,128)(2,1)S(1)} %copy-done.11), channel_id=3, replica_groups=mesh['dp'=16,'ctx'=16] {'ctx'}, dimensions={1}, use_global_device_ids=true | all-gather | bytes 278528 | tf_op jit(solution)/shard_map/all_gather | solution.py:172
  77.0 15.3 %all-gather.4.cloned.1.call-done = bf16[1,2048,512]{2,1,0:T(8,128)(2,1)} async-done(((bf16[1,128,512]{2,1,0:T(8,128)(2,1)}), bf16[1,2048,512]{2,1,0:T(8,128)(2,1)}) %all-gather.4.cloned.1.call-update) | async-done | bytes 2097168 | tf_op jit(solution)/shard_map/all_gather | solution.py:171
  92.3 10.7 %while.48 = (s32[]{:T(128)}, f32[16,128]{1,0:T(8,128)S(1)}, f32[16,128]{1,0:T(8,128)S(1)}, f32[16,128]{1,0:T(8,128)S(1)}, s32[]{:T(128)}, /*index=5*/s32[]{:T(12...) while((s32[]{:T(128)}, f32[16,128]{1,0:T(8,128)S(1)}, ...), condition=%wide.region_11.12_spmd.clone, body=%wide.region_3.11_spmd.clone.sunk | while | flops 2293450752 | bytes 35353632 | solution.py:182
  93.0 7.6 %conditional.6 = (f32[16,128]{1,0:T(8,128)S(1)}, f32[16,128]{1,0:T(8,128)S(1)}, f32[16,128]{1,0:T(8,128)S(1)}) conditional(s32[]{:T(128)} %convert_element_type.123, (s32[]{:T(128)}, s32[]{:T(128)}, s32[8]{0:T(128)S(1)}, s32[128]{0:T(128)S(1)}, bf16[2048,512]{1,0:T(8,128)(2,1)}, /*index=5*/bf16[128,16,512]{2,0,1:T(8,128)(2,1)S(1)}, ...), branch_computations={%region_4.9_spmd, %region_10.10_spmd} | conditional | flops 2293450752 | bytes 35336400 | solution.py:123
  93.0 0.2 reduce-window.25
  93.2 0.1 convert_reduce_fusion
  93.3 0.2 compare_and_fusion
  93.5 2.3 fusion.10
  95.9 0.9 fusion.5
  96.8 0.7 copy-done.5
  97.5 2.4 fusion.4
  99.9 0.7 fusion.8
  103.0 0.8 broadcast_in_dim.94
  103.9 2.5 broadcast.165.clone
  106.4 2.5 broadcast_in_dim.93
  108.9 2.5 broadcast.165
  111.4 22.7 %while.49 = (s32[]{:T(128)}, f32[128,16,512]{2,0,1:T(8,128)}, f32[128,16,64]{0,2,1:T(8,128)S(1)}, f32[128,16,512]{2,0,1:T(8,128)}, f32[2048,512]{1,0:T(8,128)}, ...) while((s32[]{:T(128)}, f32[128,16,512]{2,0,1:T(8,128)}, ...), condition=%wide.region_17.18_spmd.clone, body=%wide.region_12.0_spmd.clone.sunk | while | flops 6857830400 | bytes 153122064 | solution.py:193
  112.1 19.8 %conditional.7 = ((f32[128,16,512]{2,0,1:T(8,128)}, f32[128,16,64]{0,2,1:T(8,128)S(1)}, f32[128,16,512]{2,0,1:T(8,128)}, f32[2048,512]{1,0:T(8,128)}, f32[2048,64]{0,1:T(8,128)})) conditional(s32[]{:T(128)} %convert_element_type.124, (s32[]{:T(128)}, s32[]{:T(128)}, s32[8]{0:T(128)S(1)}, s32[128]{0:T(128)S(1)}, bf16[2048,512]{1,0:T(8,128)(2,1)}, ...), branch_computations={%region_13.15_spmd, %region_16.16_spmd} | conditional | flops 6857830400 | bytes 153121120 | solution.py:152
  112.1 0.2 reduce-window.26
  112.3 0.1 convert_reduce_fusion.1
  112.4 0.2 compare_and_fusion.1
  112.6 2.3 fusion.36
  114.9 1.2 fusion.22
  116.1 0.4 copy-done.6
  116.5 1.2 convolution_bitcast_fusion
  117.8 0.3 copy-done.7
  118.1 1.3 fusion.20
  119.4 0.9 copy-done.3
  120.3 1.5 bitcast_add_fusion
  121.8 2.5 fusion.30
  124.3 0.5 fusion.27
  124.8 3.7 fusion.26
  128.5 1.4 bitcast_add_fusion.1
  129.9 2.0 copy-done.1
  134.1 0.0 all-reduce.2.cloned.1.call-start
  134.2 3.2 convolution_bitcast_fusion.4
  137.4 0.4 copy-done.2
  137.8 0.1 copy-done.9
  137.9 0.7 convolution_bitcast_fusion.5
  138.6 4.8 pad_maximum_fusion
  143.4 8.9 %copy.66 = f32[512,4096]{1,0:T(8,128)} copy(f32[512,4096]{0,1:T(8,128)} %bitcast.133) | data formatting | bytes 16777216 | tf_op jit(solution)/shard_map/reshape | solution.py:218
  152.4 0.5 reduce-scatter.3.cloned.1.call-update
  152.9 3.6 fusion.60
  156.5 1.0 copy.67
  157.5 0.1 multiply_convert_fusion.3
  157.6 0.9 copy.68
  158.5 139.1 %reduce-scatter.5.cloned.1.call-done = f32[128,64]{0,1:T(8,128)} async-done(((f32[2048,64]{0,1:T(8,128)}), f32[128,64]{0,1:T(8,128)}) %reduce-scatter.5.cloned.1.call-update) | async-done | bytes 32784 | tf_op jit(solution)/shard_map/reduce_scatter | solution.py:198
  297.5 1.4 convert_bitcast_fusion.3
  298.9 289.6 %all-reduce.2.cloned.1.call-done = f32[512,4096]{1,0:T(8,128)} async-done(((f32[512,4096]{1,0:T(8,128)}), f32[512,4096]{1,0:T(8,128)}) %all-reduce.2.cloned.1.call-update) | async-done | bytes 8388624 | tf_op jit(solution)/shard_map/psum | solution.py:218
  588.5 1.9 constant_dynamic-slice_fusion
  590.4 100.5 %reduce-scatter.3.cloned.1.call-done = f32[128,512]{1,0:T(8,128)} async-done(((f32[2048,512]{1,0:T(8,128)}), f32[128,512]{1,0:T(8,128)}) %reduce-scatter.3.cloned.1.call-update) | async-done | bytes 262160 | tf_op jit(solution)/shard_map/reduce_scatter | solution.py:197
  690.9 1.6 convert_bitcast_fusion.2
  (57 shorter events, 0.5 us)
Async XLA Ops:
  7.2 85.1 %all-gather.4.cloned.1.call-start = ((), (), s32[]{:S(2)}) async-start(), calls=%async_computation.5 | async-start | bytes 2228224 | tf_op jit(solution)/shard_map/all_gather | solution.py:171
  7.9 289.6 %reduce-scatter.5.cloned.1.call-start = ((), (), s32[]{:S(2)}) async-start(), calls=%async_computation.3 | async-start | bytes 557056 | tf_op jit(solution)/shard_map/reduce_scatter | solution.py:198
  11.8 8.2 %copy-start.8 = (bf16[1,128,2048]{1,2,0:T(8,128)(2,1)}, bf16[1,128,2048]{1,2,0:T(8,128)(2,1)S(1)}, u32[]{:S(2)}) copy-start(bf16[1,128,2048]{1,2,0:T(8,128)(2,1)S(1)} %copy.76) | copy-start | bytes 1572868
  13.3 13.3 %copy-start.10 = (bf16[1,128,2048]{1,2,0:T(8,128)(2,1)}, bf16[1,128,2048]{1,2,0:T(8,128)(2,1)S(1)}, u32[]{:S(2)}) copy-start(bf16[1,128,2048]{1,2,0:T(8,128)(2,1)S(1)} %copy.77) | copy-start | bytes 1572868
  26.7 7.8 %copy-start.11 = (bf16[1,128,64]{1,2,0:T(8,128)(2,1)S(1)}, bf16[1,128,64]{1,2,0:T(8,128)(2,1)}, u32[]{:S(2)}) copy-start(bf16[1,128,64]{1,2,0:T(8,128)(2,1)} %param.18) | copy-start | bytes 49156
  26.7 65.6 %copy-start.12 = (s32[1,8]{1,0:T(1,128)S(1)}, s32[1,8]{1,0:T(1,128)}, u32[]{:S(2)}) copy-start(s32[1,8]{1,0:T(1,128)} %param.21) | copy-start | bytes 100
  95.9 1.6 copy-start.5
  114.9 1.6 copy-start.6
  116.5 1.6 copy-start.7
  118.1 2.2 copy-start.3
  121.8 6.8 copy-start.4
  124.8 3.7 copy-start
  129.9 2.0 copy-start.1
  134.1 454.4 %all-reduce.2.cloned.1.call-start = ((), (), s32[]{:S(2)}) async-start(), calls=%async_computation.4 | async-start | bytes 16777216 | tf_op jit(solution)/shard_map/psum | solution.py:218
  134.2 3.6 copy-start.2
  134.2 3.7 copy-start.9
  152.3 538.5 %reduce-scatter.3.cloned.1.call-start = ((), (), s32[]{:S(2)}) async-start(), calls=%async_computation.2 | async-start | bytes 4456448 | tf_op jit(solution)/shard_map/reduce_scatter | solution.py:197
Sparse Core Ops, SparseCore 0:
  9.8 82.4 all-gather.3
  134.2 163.2 reduce-scatter.4
  303.9 284.5 all-reduce.1
  590.9 99.9 reduce-scatter.2
where the time goes:
time: 703 us; the launch traced here: 699 us
  waiting for transfers between devices  546 us (78%)
  local copies, waits for them, and re-layouts  43.8 us (6%)
  blocking collectives  42.5 us (6%)
  matrix products  36.2 us (5%)
  between operations  13.9 us (2%)
  other arithmetic  10.5 us (1%)
    psum x1, waiting for transfers between devices, body(): lax.psum(joined.reshape(LATENT, HEAD_COUNT * (HEAD_DIM + VALUE_DIM)), ('d...  290 us
    reduce_scatter x1, waiting for transfers between devices, body(): lax.psum_scatter(acc_keyrot, 'ctx', scatter_dimension=0, tiled=True)  139 us
    reduce_scatter x1, waiting for transfers between devices, body(): lax.psum_scatter(acc_keys, 'ctx', scatter_dimension=0, tiled=True)  100 us
    all_gather x1, blocking collectives, body(): lax.all_gather(key_rope[0], 'ctx', axis=0, tiled=True)  42.5 us
    dot_general x17, matrix products, product(): return jnp.einsum(form, left, right, preferred_element_type=jnp.float32)  36.2 us
    unnamed x18, local copies, waits for them, and re-layouts  17 us
    all_gather x1, waiting for transfers between devices, body(): lax.all_gather(latent[0], 'ctx', axis=0, tiled=True)  15.3 us
  transfers between devices with their start and end apart: 4, of which 4 were waited for; matrix products, arithmetic and copies ran while one was open for 8% of the time, Pallas kernels for 0%

commit v1 on v0

v1 whole, which is shorter than its diff:
```python
import functools
import math

import jax
import jax.numpy as jnp
from jax import lax
from jax.experimental import pallas as pl
from jax.experimental.pallas import tpu as pltpu
from jax.sharding import PartitionSpec as P

HEADS = 16
DIM = 128
ROPE = 64
LATENT = 512
BLOCK = 128
SEQ = 2048
GROUP = 4
SCALE = (DIM + ROPE) ** -0.5
NEGATIVE = -1e30
MESH = pl.DeviceIdType.MESH
VMEM = pltpu.VMEM
F32 = jnp.float32
BF16 = jnp.bfloat16
MIB = 1 << 20


def coords():
    dp, ctx = lax.axis_index("dp"), lax.axis_index("ctx")
    return dp // 8, (dp // 2) % 4, dp % 2, ctx // 4, ctx % 4


def device(zh, y, c, x, z):
    return ((zh * 4 + y) * 2 + c, x * 4 + z)


def remote(src, dst, send, recv, target):
    return pltpu.make_async_remote_copy(
        src_ref=src, dst_ref=dst, send_sem=send, recv_sem=recv, device_id=target, device_id_type=MESH
    )


def greet(targets):
    barrier = pltpu.get_barrier_semaphore()
    for target in targets:
        pl.semaphore_signal(barrier, inc=1, device_id=target, device_id_type=MESH)
    pl.semaphore_wait(barrier, len(targets))


def dot_bt(left, right):
    return lax.dot_general(left, right, (((1,), (1,)), ((), ())), preferred_element_type=F32)


def dot(left, right):
    return jnp.dot(left, right, preferred_element_type=F32)


def gather_kernel(
    nope, rope, gout, lat, krope, lens,
    o_nope, o_gout, o_rope, o_keys, o_lens,
    kblk, q_send, q_recv, kx_send, kx_recv, kz_send, kz_recv, ks_send, ks_recv, l_sem, loc,
):
    zh, y, c, x, z = coords()
    s = x // 2
    sib = device(zh, y, 1 - c, x, z)
    others = [device(zh, y, c, (x + d) % 4, z) for d in (1, 2, 3)]
    others += [device(zh, y, 1 - c, (x + d) % 4, z) for d in (0, 1, 2, 3)]
    others += [device(zh, y, c, x, (z + d) % 4) for d in (1, 2, 3)]
    kblk[:, 0:LATENT] = lat[...]
    pair = krope[...]
    kblk[:, LATENT:LATENT + 2 * ROPE] = jnp.concatenate([pair, pair], axis=1)
    greet(others)

    def rows(at):
        return pl.ds(pl.multiple_of(at * BLOCK, BLOCK), BLOCK)

    home = 4 * x + z

    def key_send(t):
        return remote(kblk, o_keys.at[rows(home)], kx_send.at[t], kx_recv.at[x // 2], device(zh, y, x % 2, 2 * c + t, z))

    def key_local():
        return pltpu.make_async_copy(kblk, o_keys.at[rows(home)], loc.at[0])

    key_self = [(2 * c + t == x) & (x % 2 == c) for t in (0, 1)]
    for t in (0, 1):
        @pl.when(jnp.logical_not(key_self[t]))
        def _():
            key_send(t).start()

        @pl.when(key_self[t])
        def _():
            key_local().start()

    def q_copies(g, target):
        wide = pl.ds(g * GROUP * DIM, GROUP * DIM)
        thin = pl.ds(g * GROUP * ROPE, GROUP * ROPE)
        return [
            remote(nope.at[:, wide], o_nope.at[rows(x)], q_send.at[0, g], q_recv.at[0, x], target),
            remote(gout.at[:, wide], o_gout.at[rows(x)], q_send.at[1, g], q_recv.at[1, x], target),
            remote(rope.at[:, thin], o_rope.at[rows(x)], q_send.at[2, g], q_recv.at[2, x], target),
        ]

    def q_local(g):
        wide = pl.ds(g * GROUP * DIM, GROUP * DIM)
        thin = pl.ds(g * GROUP * ROPE, GROUP * ROPE)
        return [
            pltpu.make_async_copy(nope.at[:, wide], o_nope.at[rows(x)], loc.at[1]),
            pltpu.make_async_copy(gout.at[:, wide], o_gout.at[rows(x)], loc.at[2]),
            pltpu.make_async_copy(rope.at[:, thin], o_rope.at[rows(x)], loc.at[3]),
        ]

    q_self = [(2 * c + g // 2 == x) & (c == g % 2) for g in range(4)]
    for g in range(4):
        @pl.when(jnp.logical_not(q_self[g]))
        def _():
            for copy in q_copies(g, device(zh, y, g % 2, 2 * c + g // 2, z)):
                copy.start()

        @pl.when(q_self[g])
        def _():
            for copy in q_local(g):
                copy.start()

    lens_copy = remote(lens, o_lens, l_sem.at[0], l_sem.at[1], sib)
    lens_copy.start()

    def z_copy(k, d):
        at = rows(4 * (c + 2 * k) + z)
        return remote(o_keys.at[at], o_keys.at[at], kz_send.at[k, d - 1], kz_recv.at[k, d - 1], device(zh, y, c, x, (z + d) % 4))

    def sib_copy(k, d):
        at = rows(4 * (c + 2 * k) + (z + 4 - d) % 4)
        return remote(o_keys.at[at], o_keys.at[at], ks_send.at[k, d], ks_recv.at[k, d], sib)

    for k in (0, 1):
        own = c + 2 * k
        self_here = (own == x) & (s == c)

        @pl.when(jnp.logical_not(self_here))
        def _():
            remote(kblk, o_keys.at[rows(4 * own + z)], kx_send.at[0], kx_recv.at[k], sib).wait_recv()

        @pl.when(self_here)
        def _():
            key_local().wait()

        for d in (1, 2, 3):
            z_copy(k, d).start()
        sib_copy(k, 0).start()

    def z_arrival(k, d):
        at = rows(4 * (c + 2 * k) + (z + 4 - d) % 4)
        return remote(o_keys.at[at], o_keys.at[at], kz_send.at[k, d - 1], kz_recv.at[k, d - 1], device(zh, y, c, x, (z + 4 - d) % 4))

    def sib_arrival(k, d):
        at = rows(4 * (1 - c + 2 * k) + (z + 4 - d) % 4)
        return remote(o_keys.at[at], o_keys.at[at], ks_send.at[k, d], ks_recv.at[k, d], sib)

    for d in (1, 3, 2):
        for k in (0, 1):
            z_arrival(k, d).wait_recv()
            sib_copy(k, d).start()
    for d in (0, 1, 3, 2):
        for k in (0, 1):
            sib_arrival(k, d).wait_recv()

    for xs in range(4):
        self_here = (xs == x) & (s == c)

        @pl.when(jnp.logical_not(self_here))
        def _():
            at = rows(xs)
            remote(nope.at[:, 0:GROUP * DIM], o_nope.at[at], q_send.at[0, 0], q_recv.at[0, xs], sib).wait_recv()
            remote(gout.at[:, 0:GROUP * DIM], o_gout.at[at], q_send.at[1, 0], q_recv.at[1, xs], sib).wait_recv()
            remote(rope.at[:, 0:GROUP * ROPE], o_rope.at[at], q_send.at[2, 0], q_recv.at[2, xs], sib).wait_recv()
    for g in range(4):
        @pl.when(q_self[g])
        def _():
            for copy in q_local(g):
                copy.wait()

        @pl.when(jnp.logical_not(q_self[g]))
        def _():
            for copy in q_copies(g, sib):
                copy.wait_send()
    for t in (0, 1):
        @pl.when(jnp.logical_not(key_self[t]))
        def _():
            key_send(t).wait_send()
    for k in (0, 1):
        for d in (1, 2, 3):
            z_copy(k, d).wait_send()
        for d in (0, 1, 2, 3):
            sib_copy(k, d).wait_send()
    lens_copy.wait()


CHUNK = 256
PAIR = 2 * BLOCK


def fold(values, op):
    return op(values.reshape(values.shape[0] // 8, 8, values.shape[1]), axis=0)


def attend_kernel(
    lens, qn, go, qr, keys, w,
    o_qn, o_qr, o_keys, o_w,
    kx, vx, ktx, qx, st, dpt, dkv, dkr, dqt, latt,
):
    ctx = lax.axis_index("ctx")
    z = ctx % 4
    chunk = 512
    lane = lax.broadcasted_iota(jnp.int32, (1, 2 * ROPE), 1)

    for h in range(GROUP):
        qx[:, h * 256:h * 256 + DIM] = qn[:, h * DIM:(h + 1) * DIM]
        half = qr[:, (h // 2) * 128:(h // 2) * 128 + 128]
        keep = (lane < ROPE) if h % 2 == 0 else (lane >= ROPE)
        qx[:, h * 256 + DIM:(h + 1) * 256] = jnp.where(keep, half, jnp.zeros_like(half))
    wt = [w[:, h * 256:h * 256 + DIM].T for h in range(GROUP)]

    def project(i, carry):
        at = pl.ds(pl.multiple_of(i * chunk, chunk), chunk)
        rows = keys[at, 0:LATENT]
        rot = keys[at, LATENT:LATENT + 128]
        rot_t = rot.T
        for h in range(GROUP):
            both = dot(rows, w[:, h * 256:(h + 1) * 256]).astype(BF16)
            kx[at, h * 256:h * 256 + DIM] = both[:, 0:DIM]
            kx[at, h * 256 + DIM:(h + 1) * 256] = rot
            vx[at, h * DIM:(h + 1) * DIM] = both[:, DIM:256]
            ktx[h, 0:DIM, at] = dot_bt(wt[h], rows).astype(BF16)
            ktx[h, DIM:256, at] = rot_t
        latt[:, at] = rows.T
        dkv[at, :] = jnp.zeros((chunk, GROUP * 256), BF16)
        dkr[at, :] = jnp.zeros((chunk, 128), F32)
        return carry

    lax.fori_loop(0, SEQ // chunk, project, 0)

    row_lane = lax.broadcasted_iota(jnp.int32, (1, PAIR), 1)
    for t in (1, 0):
        at_rows = slice(t * PAIR, (t + 1) * PAIR)
        pos = (4 * (2 * t + row_lane // BLOCK) + z) * BLOCK + row_lane % BLOCK
        first_pos = (8 * t + z) * BLOCK
        start = jnp.zeros_like(pos)
        floor = jnp.int32(0)
        end = jnp.int32(0)
        for d in range(8):
            end = end + lens[d]
            start = jnp.maximum(start, jnp.where(end <= pos, end, 0))
            floor = jnp.maximum(floor, jnp.where(end <= first_pos, end, 0))
        low = floor // CHUNK
        high = (8 * t + 6 + z) // 2

        def scores(i, carry):
            at = pl.ds(pl.multiple_of(i * CHUNK, CHUNK), CHUNK)
            key = lax.broadcasted_iota(jnp.int32, (CHUNK, PAIR), 0) + i * CHUNK
            seen = (key <= pos) & (key >= start)
            out = []
            for h in range(GROUP):
                s = dot_bt(kx[at, h * 256:(h + 1) * 256], qx[at_rows, h * 256:(h + 1) * 256])
                s = jnp.where(seen, s * (SCALE * math.log2(math.e)), NEGATIVE)
                st[h, at, :] = s
                out.append(jnp.maximum(carry[h], fold(s, jnp.max)))
            return tuple(out)

        tops = lax.fori_loop(low, high, scores, tuple(jnp.full((8, PAIR), NEGATIVE, F32) for h in range(GROUP)))
        top = [jnp.max(tops[h], axis=0, keepdims=True) for h in range(GROUP)]

        def sums(i, carry):
            at = pl.ds(pl.multiple_of(i * CHUNK, CHUNK), CHUNK)
            out = []
            for h in range(GROUP):
                p = jnp.exp2(st[h, at, :] - top[h])
                d = dot_bt(vx[at, h * DIM:(h + 1) * DIM], go[at_rows, h * DIM:(h + 1) * DIM])
                st[h, at, :] = p
                dpt[h, at, :] = d
                out.append(carry[2 * h] + fold(p, jnp.sum))
                out.append(carry[2 * h + 1] + fold(p * d, jnp.sum))
            return tuple(out)

        totals = lax.fori_loop(low, high, sums, tuple(jnp.zeros((8, PAIR), F32) for h in range(2 * GROUP)))
        inv = [1.0 / jnp.sum(totals[2 * h], axis=0, keepdims=True) for h in range(GROUP)]
        inner = [jnp.sum(totals[2 * h + 1], axis=0, keepdims=True) * inv[h] for h in range(GROUP)]
        for h in range(GROUP):
            dqt[h] = jnp.zeros((256, PAIR), F32)

        def grads(i, carry):
            at = pl.ds(pl.multiple_of(i * CHUNK, CHUNK), CHUNK)
            rot = dkr[at, :]
            for h in range(GROUP):
                p = st[h, at, :] * inv[h]
                ds = ((p * SCALE) * (dpt[h, at, :] - inner[h])).astype(BF16)
                low_p = p.astype(BF16)
                dk = dot(ds, qx[at_rows, h * 256:(h + 1) * 256])
                dv = dot(low_p, go[at_rows, h * DIM:(h + 1) * DIM])
                dqt[h] += dot(ktx[h, :, at], ds)
                rot = rot + dk[:, DIM:256]
                both = jnp.concatenate([dk[:, 0:DIM], dv], axis=1)
                if t == 0:
                    both = both + dkv[at, h * 256:(h + 1) * 256].astype(F32)
                dkv[at, h * 256:(h + 1) * 256] = both.astype(BF16)
            dkr[at, :] = rot
            return carry

        lax.fori_loop(low, high, grads, 0)
        rots = []
        for h in range(GROUP):
            dq = dqt[h].T
            o_qn[at_rows, h * DIM:(h + 1) * DIM] = dq[:, 0:DIM].astype(BF16)
            rots.append(dq[:, DIM:256])
        for p in (0, 1):
            o_qr[at_rows, p * 128:(p + 1) * 128] = jnp.where(lane < ROPE, rots[2 * p], rots[2 * p + 1]).astype(BF16)

    def back(i, carry):
        at = pl.ds(pl.multiple_of(i * chunk, chunk), chunk)
        o_keys[at, 0:LATENT] = dot_bt(dkv[at, :], w[...]).astype(BF16)
        rot = dkr[at, :]
        o_keys[at, LATENT:LATENT + 128] = (rot + pltpu.roll(rot, ROPE, 1)).astype(BF16)
        return carry

    lax.fori_loop(0, SEQ // chunk, back, 0)
    for n in range(GROUP):
        o_w[:, n * 256:(n + 1) * 256] = dot(latt[...], dkv[:, n * 256:(n + 1) * 256]).astype(BF16)


def reduce_kernel(
    dqn, dqr, dkp, wp,
    o_qn, o_qr, o_lat, o_rot, o_w,
    sin, acc, zin, fin, hin, yin, ys, cin, cs, hi_in, fs, ag,
    q_send, q_recv, s_send, s_recv, z_send, z_recv, h_send, h_recv, y_send, y_recv, c_send, c_recv, hi_sem, a_send, a_recv, loc,
):
    zh, y, c, x, z = coords()
    s = x // 2
    g = 2 * (x % 2) + c
    ctx = 4 * x + z
    sib = device(zh, y, 1 - c, x, z)
    others = [device(zh, y, c, (x + dx) % 4, (z + dz) % 4) for dx in range(4) for dz in range(4) if dx or dz]
    others += [device(zh, y, 1 - c, (x + d) % 4, z) for d in range(4)]
    others += [device(zh, (y + d) % 4, cc, x, z) for d in (1, 2, 3) for cc in (0, 1)]
    others += [device(1 - zh, y, c, x, z)]
    greet(others)

    def rows(at, size=BLOCK):
        return pl.ds(pl.multiple_of(at * BLOCK, BLOCK), size)

    def s_copy(k):
        return remote(dkp.at[rows(4 * (1 - c + 2 * k), 512)], sin.at[k], s_send.at[k], s_recv.at[k], sib)

    for k in (0, 1):
        s_copy(k).start()

    def y_copy(d):
        peer = (y + d) % 4
        return remote(wp.at[:, pl.ds(pl.multiple_of(peer * 256, 256), 256)], yin.at[d - 1], y_send.at[d - 1], y_recv.at[d - 1], device(zh, peer, c, x, z))

    for d in (1, 3, 2):
        y_copy(d).start()

    def q_copies(xs):
        target = device(zh, y, s, xs, z)
        at = rows(xs)
        wide = pl.ds(pl.multiple_of(g * GROUP * DIM, GROUP * DIM), GROUP * DIM)
        thin = pl.ds(pl.multiple_of(g * GROUP * ROPE, GROUP * ROPE), GROUP * ROPE)
        return [
            remote(dqn.at[at], o_qn.at[:, wide], q_send.at[0, xs], q_recv.at[0, g], target),
            remote(dqr.at[at], o_qr.at[:, thin], q_send.at[1, xs], q_recv.at[1, g], target),
        ]

    def q_local():
        at = rows(x)
        wide = pl.ds(pl.multiple_of(g * GROUP * DIM, GROUP * DIM), GROUP * DIM)
        thin = pl.ds(pl.multiple_of(g * GROUP * ROPE, GROUP * ROPE), GROUP * ROPE)
        return [
            pltpu.make_async_copy(dqn.at[at], o_qn.at[:, wide], loc.at[0]),
            pltpu.make_async_copy(dqr.at[at], o_qr.at[:, thin], loc.at[1]),
        ]

    q_self = [(xs == x) & (s == c) for xs in range(4)]
    for xs in range(4):
        @pl.when(jnp.logical_not(q_self[xs]))
        def _():
            for copy in q_copies(xs):
                copy.start()

        @pl.when(q_self[xs])
        def _():
            for copy in q_local():
                copy.start()

    def z_copy(k, d):
        peer = (z + d) % 4
        return remote(acc.at[k, rows(peer)], zin.at[d - 1, k], z_send.at[k, d - 1], z_recv.at[k, d - 1], device(zh, y, c, x, peer))

    for k in (0, 1):
        s_copy(k).wait_recv()
        acc[k] = (dkp[rows(4 * (c + 2 * k), 512), :].astype(F32) + sin[k].astype(F32)).astype(BF16)
        for d in (2, 1, 3):
            z_copy(k, d).start()

    for d in (1, 3, 2):
        y_copy(d).wait_recv()
    mine = wp[:, pl.ds(pl.multiple_of(y * 256, 256), 256)].astype(F32)
    ys[...] = (mine + yin[0].astype(F32) + yin[1].astype(F32) + yin[2].astype(F32)).astype(BF16)

    def c_copy(dx, dz):
        px, pz = (x + dx) % 4, (z + dz) % 4
        src = ys.at[pl.ds(pl.multiple_of((4 * px + pz) * 32, 32), 32)]
        return remote(src, cin.at[dx, dz], c_send.at[dx, dz], c_recv.at[dx, dz], device(zh, y, c, px, pz))

    pairs = [(dx, dz) for dz in (2, 1, 3, 0) for dx in (2, 1, 3, 0) if dx or dz]
    for dx, dz in pairs:
        c_copy(dx, dz).start()

    def h_copy(k):
        return remote(fin.at[k], hin.at[x % 2], h_send.at[k], h_recv.at[x % 2], device(zh, y, s, c + 2 * k, z))

    def h_local(k):
        return pltpu.make_async_copy(fin.at[k], hin.at[x % 2], loc.at[2])

    h_self = [(c + 2 * k == x) & (s == c) for k in (0, 1)]
    for k in (0, 1):
        for d in (1, 3, 2):
            z_copy(k, d).wait_recv()
        total = acc[k, rows(z), :].astype(F32)
        for d in (1, 2, 3):
            total = total + zin[d - 1, k].astype(F32)
        fin[k] = total.astype(BF16)

        @pl.when(jnp.logical_not(h_self[k]))
        def _():
            h_copy(k).start()

        @pl.when(h_self[k])
        def _():
            h_local(k).start()

    for dx, dz in pairs:
        c_copy(dx, dz).wait_recv()
    own = ys[pl.ds(pl.multiple_of(ctx * 32, 32), 32), :].astype(F32)
    even = own
    for dz in (1, 2, 3):
        even = even + cin[0, dz].astype(F32)
    for dz in range(4):
        even = even + cin[2, dz].astype(F32)
    odd = jnp.zeros_like(own)
    for dx in (1, 3):
        for dz in range(4):
            odd = odd + cin[dx, dz].astype(F32)
    flip = x % 2 == 1
    cs[:, 0:256] = jnp.where(flip, odd, even).astype(BF16)
    cs[:, 256:512] = jnp.where(flip, even, odd).astype(BF16)
    hi_copy = remote(cs, hi_in, hi_sem.at[0], hi_sem.at[1], device(1 - zh, y, c, x, z))
    hi_copy.start()

    for t in (0, 1):
        self_here = (2 * c + t == x) & (x % 2 == c)

        @pl.when(jnp.logical_not(self_here))
        def _():
            remote(fin.at[0], hin.at[t], h_send.at[0], h_recv.at[t], sib).wait_recv()
    for k in (0, 1):
        @pl.when(h_self[k])
        def _():
            h_local(k).wait()
    final = hin[0].astype(F32) + hin[1].astype(F32)
    o_lat[...] = final[:, 0:LATENT].astype(BF16)
    o_rot[...] = final[:, LATENT:LATENT + ROPE].astype(BF16)

    hi_copy.wait_recv()
    fs[...] = (cs[...].astype(F32) + hi_in[...].astype(F32)).astype(BF16)

    def a_copy(dy, dc):
        peer = device(zh, (y + dy) % 4, (c + dc) % 2, x, z)
        return remote(fs, ag.at[dy, dc], a_send.at[dy, dc], a_recv.at[dy, dc], peer)

    members = [(dy, dc) for dy in (2, 1, 3, 0) for dc in (0, 1) if dy or dc]
    for dy, dc in members:
        a_copy(dy, dc).start()

    def place(values, from_y, from_c):
        wide = values.astype(F32)
        for p in (0, 1):
            at = pl.multiple_of((2 * p + from_c) * 1024 + from_y * 256, 256)
            o_w[:, pl.ds(at, 256)] = wide[:, p * 256:(p + 1) * 256]

    place(fs[...], y, c)
    for dy, dc in members:
        a_copy(dy, dc).wait_recv()
        place(ag[dy, dc], (y + 4 - dy) % 4, (c + dc) % 2)

    for gs in range(4):
        self_here = (g == gs) & (s == c)

        @pl.when(jnp.logical_not(self_here))
        def _():
            remote(dqn.at[0:BLOCK], o_qn.at[:, gs * GROUP * DIM:(gs + 1) * GROUP * DIM], q_send.at[0, 0], q_recv.at[0, gs], sib).wait_recv()
            remote(dqr.at[0:BLOCK], o_qr.at[:, gs * GROUP * ROPE:(gs + 1) * GROUP * ROPE], q_send.at[1, 0], q_recv.at[1, gs], sib).wait_recv()
    for xs in range(4):
        @pl.when(jnp.logical_not(q_self[xs]))
        def _():
            for copy in q_copies(xs):
                copy.wait_send()

        @pl.when(q_self[xs])
        def _():
            for copy in q_local():
                copy.wait()
    for k in (0, 1):
        s_copy(k).wait_send()
        for d in (1, 2, 3):
            z_copy(k, d).wait_send()

        @pl.when(jnp.logical_not(h_self[k]))
        def _():
            h_copy(k).wait_send()
    for d in (1, 2, 3):
        y_copy(d).wait_send()
    for dx, dz in pairs:
        c_copy(dx, dz).wait_send()
    hi_copy.wait_send()
    for dy, dc in members:
        a_copy(dy, dc).wait_send()


def vmem():
    return pl.BlockSpec(memory_space=pltpu.VMEM)


def shape(dims, kind=BF16):
    return jax.ShapeDtypeStruct(dims, kind)


def dma(*dims):
    return pltpu.SemaphoreType.DMA(dims)


def gather(nope, rope, gout, lat, krope, lens):
    return pl.pallas_call(
        gather_kernel,
        name="gather_rows",
        out_shape=(
            shape((512, GROUP * DIM)),
            shape((512, GROUP * DIM)),
            shape((512, GROUP * ROPE)),
            shape((SEQ, LATENT + 128)),
            shape((8, 128), jnp.int32),
        ),
        in_specs=[vmem()] * 6,
        out_specs=(vmem(),) * 5,
        scratch_shapes=[
            VMEM((BLOCK, LATENT + 128), BF16),
            dma(3, 4), dma(3, 4), dma(2), dma(2), dma(2, 3), dma(2, 3), dma(2, 4), dma(2, 4), dma(2), dma(4),
        ],
        compiler_params=pltpu.CompilerParams(collective_id=0, has_side_effects=True, vmem_limit_bytes=24 * MIB),
    )(nope, rope, gout, lat, krope, lens)


def attend(lens, qn, go, qr, keys, w):
    return pl.pallas_call(
        attend_kernel,
        name="attend_rows",
        out_shape=(
            shape((512, GROUP * DIM)),
            shape((512, GROUP * ROPE)),
            shape((SEQ, LATENT + 128)),
            shape((LATENT, GROUP * 256)),
        ),
        in_specs=[pl.BlockSpec(memory_space=pltpu.SMEM)] + [vmem()] * 5,
        out_specs=(vmem(),) * 4,
        scratch_shapes=[
            VMEM((SEQ, GROUP * 256), BF16),
            VMEM((SEQ, GROUP * DIM), BF16),
            VMEM((GROUP, 256, SEQ), BF16),
            VMEM((512, GROUP * 256), BF16),
            VMEM((GROUP, SEQ, PAIR), F32),
            VMEM((GROUP, SEQ, PAIR), F32),
            VMEM((SEQ, GROUP * 256), BF16),
            VMEM((SEQ, 128), F32),
            VMEM((GROUP, 256, PAIR), F32),
            VMEM((LATENT, SEQ), BF16),
        ],
        compiler_params=pltpu.CompilerParams(vmem_limit_bytes=56 * MIB),
    )(lens, qn, go, qr, keys, w)


def reduce(dqn, dqr, dkp, wp):
    return pl.pallas_call(
        reduce_kernel,
        name="reduce_rows",
        out_shape=(
            shape((BLOCK, HEADS * DIM)),
            shape((BLOCK, HEADS * ROPE)),
            shape((BLOCK, LATENT)),
            shape((BLOCK, ROPE)),
            shape((32, HEADS * 256), F32),
        ),
        in_specs=[vmem()] * 4,
        out_specs=(vmem(),) * 5,
        scratch_shapes=[
            VMEM((2, 512, 640), BF16),
            VMEM((2, 512, 640), BF16),
            VMEM((3, 2, BLOCK, 640), BF16),
            VMEM((2, BLOCK, 640), BF16),
            VMEM((2, BLOCK, 640), BF16),
            VMEM((3, 512, 256), BF16),
            VMEM((512, 256), BF16),
            VMEM((4, 4, 32, 256), BF16),
            VMEM((32, 512), BF16),
            VMEM((32, 512), BF16),
            VMEM((32, 512), BF16),
            VMEM((4, 2, 32, 512), BF16),
            dma(2, 4), dma(2, 4), dma(2), dma(2), dma(2, 3), dma(2, 3), dma(2), dma(2), dma(3), dma(3),
            dma(4, 4), dma(4, 4), dma(2), dma(4, 2), dma(4, 2), dma(3),
        ],
        compiler_params=pltpu.CompilerParams(collective_id=1, has_side_effects=True, vmem_limit_bytes=40 * MIB),
    )(dqn, dqr, dkp, wp)


def body(query_nope, query_rope, latent, key_rope, grad_output, kv_up, doc_lengths):
    dp, ctx = lax.axis_index("dp"), lax.axis_index("ctx")
    c, x = dp % 2, ctx // 4
    own = jnp.pad(doc_lengths, ((0, 7), (0, 120)))
    qn, go, qr, keys, other = gather(query_nope[0], query_rope[0], grad_output[0], latent[0], key_rope[0], own)
    lens = jnp.where(x // 2 == c, own[0, :8], other[0, :8])
    g = 2 * (x % 2) + c
    w = lax.dynamic_slice_in_dim(kv_up, g * GROUP * 256, GROUP * 256, 1)
    dqn, dqr, dkp, wp = attend(lens, qn, go, qr, keys, w)
    gqn, gqr, glat, grot, gw = reduce(dqn, dqr, dkp, wp)
    return gqn[None], gqr[None], glat[None], grot[None], gw


def solution(mesh):
    rows = P("dp", "ctx", None)
    return jax.shard_map(
        body,
        mesh=mesh,
        in_specs=(rows, rows, rows, rows, rows, P(), P("dp", None)),
        out_specs=(rows, rows, rows, rows, P("ctx", None)),
        check_vma=False,
    )
```

time: 703 us -> 149 us (0.21)
  waiting for transfers between devices: 546 us -> 0 us
  Pallas kernels: 0 us -> 127 us
  blocking collectives: 42.5 us -> 0 us
  matrix products: 36.2 us -> 0 us
  local copies, waits for them, and re-layouts: 43.8 us -> 20.1 us
  between operations: 13.9 us -> 0.73 us
  other arithmetic: 10.5 us -> 0.52 us
    psum x1 -> x0, waiting for transfers between devices: 290 us -> none  [body(): lax.psum(joined.reshape(LATENT, HEAD_COUNT * (HEAD_DIM + VALUE_DIM)), ('d...]
    reduce_scatter x2 -> x0, waiting for transfers between devices: 240 us -> none  [the longest x1 139 us: body(): lax.psum_scatter(acc_keyrot, 'ctx', scatter_dimension=0, tiled=True)]
    pallas_call x0 -> x3, Pallas kernels: none -> 127 us  [the longest x1 62.5 us: reduce(): pl.pallas_call(reduce_kernel, name='reduce_rows', out_shape=(shape((BLOCK...]
    all_gather x1 -> x0, blocking collectives: 42.5 us -> none  [body(): lax.all_gather(key_rope[0], 'ctx', axis=0, tiled=True)]
    dot_general x17 -> x0, matrix products: 36.2 us -> none  [product(): return jnp.einsum(form, left, right, preferred_element_type=jnp.float32)]
    all_gather x1 -> x0, waiting for transfers between devices: 15.3 us -> none  [body(): lax.all_gather(latent[0], 'ctx', axis=0, tiled=True)]
    reshape x1 -> x0, local copies, waits for them, and re-layouts: 8.94 us -> none  [body(): joined.reshape(LATENT, HEAD_COUNT * (HEAD_DIM + VALUE_DIM))]
    another operation x6 -> x0, local copies, waits for them, and re-layouts: 7.78 us -> none
  transfers between devices with their start and end apart: 4 -> 0, of which waited for: 4 -> 0; matrix products, arithmetic and copies ran while one was open for 8% -> 0% of each run, Pallas kernels for 0% -> 0%
where the time goes in v1:
time: 149 us
  Pallas kernels  127 us (85%)
  local copies, waits for them, and re-layouts  20.1 us (13%)
    pallas_call x1, Pallas kernels, reduce(): pl.pallas_call(reduce_kernel, name='reduce_rows', out_shape=(shape((BLOCK...  62.5 us
    pallas_call x1, Pallas kernels, gather(): pl.pallas_call(gather_kernel, name='gather_rows', out_shape=(shape((512,...  36.9 us
    pallas_call x1, Pallas kernels, attend(): pl.pallas_call(attend_kernel, name='attend_rows', out_shape=(shape((512,...  27.9 us
    unnamed x30, local copies, waits for them, and re-layouts  17.1 us

profile of v1, /device:TPU:1, one launch (start us, length us, event | category | flops | bytes accessed | tf_op | source)
XLA Modules:
  0.0 148.7 jit_solution(452909016238022124)
XLA Ops:
  0.7 0.7 pad.4.lens
  1.4 0.8 copy.12
  2.2 2.3 %constant_dynamic-slice_fusion.w = bf16[512,1024]{1,0:T(8,128)(2,1)} fusion(bf16[512,4096]{1,0:T(8,128)(2,1)} %param.12, s32[]{:T(128)S(6)} %select_n.38), kind=kLoop, calls=%fused_computation.2 | loop fusion | bytes 2097156 | tf_op jit(solution)/shard_map/dynamic_slice | solution.py:629
  4.5 0.0 copy-start.3
  4.5 1.0 copy-done.3
  5.5 0.0 copy-start.4
  5.5 1.0 copy-done.4
  6.6 0.0 copy-start.10
  6.6 0.9 copy-done.10
  7.5 0.0 copy-start.11
  7.5 0.9 copy-done.11
  8.4 36.9 %gather_rows.1 = (bf16[512,512]{1,0:T(8,128)(2,1)S(1)}, bf16[512,512]{1,0:T(8,128)(2,1)S(1)}, bf16[512,256]{1,0:T(8,128)(2,1)S(1)}, bf16[2048,640]{1,0:T(8,128)(2,1)S(1)}, s32[8,128]{1,0:T(8,128)S(1)}) custom-call(bf16[128,2048]{1,0:T(8,128)(2,1)S(1)} %bitcast.11, bf16[128,1024]{1,0:T(8,128)(2,1)S(1)} %bitcast.15, bf16[128,2048]{1,0:T(8,128)(2,1)S(1)} %bitcast.12, ...), custom_call_target="tpu_custom_call" | custom-call | tf_op jit(solution)/shard_map/gather_rows/pallas_call | solution.py:541
  45.3 0.0 copy-start
  45.4 1.5 %copy-done = bf16[2048,640]{1,0:T(8,128)(2,1)} copy-done((bf16[2048,640]{1,0:T(8,128)(2,1)}, bf16[2048,640]{1,0:T(8,128)(2,1)S(1)}, u32[]{:S(2)}) %copy-start) | copy-done | bytes 2621464
  46.8 0.0 copy-start.6
  46.8 0.8 copy-done.6
  47.6 0.0 copy-start.7
  47.6 0.8 copy-done.7
  48.4 0.0 copy-start.9
  48.4 0.7 copy-done.9
  49.1 0.5 fusion.lens
  49.7 27.9 %attend_rows.1 = (bf16[512,512]{1,0:T(8,128)(2,1)}, bf16[512,256]{1,0:T(8,128)(2,1)}, bf16[2048,640]{1,0:T(8,128)(2,1)}, bf16[512,1024]{1,0:T(8,128)(2,1)}) custom-call(s32[8]{0:T(128)} %fusion.lens, bf16[512,512]{1,0:T(8,128)(2,1)} %copy-done.6, bf16[512,512]{1,0:T(8,128)(2,1)} %copy-done.7, bf16[512,256]{1,0:T(8,128)(2,1)} %copy-done.9, ...), custom_call_target="tpu_custom_call" | custom-call | tf_op jit(solution)/shard_map/attend_rows/pallas_call | solution.py:562
  77.6 0.0 copy-start.1
  77.6 1.7 %copy-done.1 = bf16[2048,640]{1,0:T(8,128)(2,1)S(1)} copy-done((bf16[2048,640]{1,0:T(8,128)(2,1)S(1)}, bf16[2048,640]{1,0:T(8,128)(2,1)}, u32[]{:S(2)}) %copy-start.1) | copy-done | bytes 2621464
  79.3 0.0 copy-start.2
  79.3 1.2 copy-done.2
  80.6 0.0 copy-start.5
  80.6 1.0 copy-done.5
  81.6 0.0 copy-start.8
  81.6 0.9 copy-done.8
  82.5 62.5 %reduce_rows.1 = (bf16[128,2048]{1,0:T(8,128)(2,1)S(1)}, bf16[128,1024]{1,0:T(8,128)(2,1)S(1)}, bf16[128,512]{1,0:T(8,128)(2,1)S(1)}, bf16[128,64]{1,0:T(8,128)(2,1)S(1)}, f32[32,4096]{1,0:T(8,128)S(1)}) custom-call(bf16[512,512]{1,0:T(8,128)(2,1)S(1)} %copy-done.5, bf16[512,256]{1,0:T(8,128)(2,1)S(1)} %copy-done.8, bf16[2048,640]{1,0:T(8,128)(2,1)S(1)} %copy-done.1, ...), custom_call_target="tpu_custom_call" | custom-call | tf_op jit(solution)/shard_map/reduce_rows/pallas_call | solution.py:590
  145.1 0.7 copy.13
  145.8 0.8 copy.18
  146.6 0.7 copy.19
  147.3 0.7 copy.20
  147.9 0.8 copy.21
Async XLA Ops:
  4.5 1.0 copy-start.3
  5.5 1.0 copy-start.4
  6.6 0.9 copy-start.10
  7.5 0.9 copy-start.11
  45.3 1.5 %copy-start = (bf16[2048,640]{1,0:T(8,128)(2,1)}, bf16[2048,640]{1,0:T(8,128)(2,1)S(1)}, u32[]{:S(2)}) copy-start(bf16[2048,640]{1,0:T(8,128)(2,1)S(1)} %get-tuple-element.23.keys) | copy-start | bytes 7864324
  46.8 0.8 copy-start.6
  47.6 0.8 copy-start.7
  48.4 0.7 copy-start.9
  77.6 1.7 %copy-start.1 = (bf16[2048,640]{1,0:T(8,128)(2,1)S(1)}, bf16[2048,640]{1,0:T(8,128)(2,1)}, u32[]{:S(2)}) copy-start(bf16[2048,640]{1,0:T(8,128)(2,1)} %get-tuple-element.26.dkp) | copy-start | bytes 7864324
  79.3 1.2 copy-start.2
  80.6 1.0 copy-start.5
  81.6 0.9 copy-start.8

commit v2 on v1

v2 whole, which is shorter than its diff:
```python
import functools
import math

import jax
import jax.numpy as jnp
from jax import lax
from jax.experimental import pallas as pl
from jax.experimental.pallas import tpu as pltpu
from jax.sharding import PartitionSpec as P

HEADS = 16
DIM = 128
ROPE = 64
LATENT = 512
BLOCK = 128
SEQ = 2048
GROUP = 4
SCALE = (DIM + ROPE) ** -0.5
NEGATIVE = -1e30
MESH = pl.DeviceIdType.MESH
VMEM = pltpu.VMEM
F32 = jnp.float32
BF16 = jnp.bfloat16
MIB = 1 << 20


def coords():
    dp, ctx = lax.axis_index("dp"), lax.axis_index("ctx")
    return dp // 8, (dp // 2) % 4, dp % 2, ctx // 4, ctx % 4


def device(zh, y, c, x, z):
    return ((zh * 4 + y) * 2 + c, x * 4 + z)


def remote(src, dst, send, recv, target):
    return pltpu.make_async_remote_copy(
        src_ref=src, dst_ref=dst, send_sem=send, recv_sem=recv, device_id=target, device_id_type=MESH
    )


def greet(targets):
    barrier = pltpu.get_barrier_semaphore()
    for target in targets:
        pl.semaphore_signal(barrier, inc=1, device_id=target, device_id_type=MESH)
    pl.semaphore_wait(barrier, len(targets))


def dot_bt(left, right):
    return lax.dot_general(left, right, (((1,), (1,)), ((), ())), preferred_element_type=F32)


def dot(left, right):
    return jnp.dot(left, right, preferred_element_type=F32)


PAIR = 2 * BLOCK
WIDE = 4 * BLOCK
HALF = BLOCK // 2
KEYS = LATENT + 2 * ROPE


def fold(values, op):
    return op(values.reshape(values.shape[0] // 8, 8, values.shape[1]), axis=0)


def across(a, p):
    return (a % 2 + p % 2) % 2 + 2 * ((a // 2 + p // 2) % 2)


def kernel(
    nope, rope, gout, lat, krope, lens, kv_up,
    o_qn, o_qr, o_lat, o_rot, o_w,
    kblk, w, qn, go, qr, own_lens, other_lens, keys, zstage,
    kx, vx, ktx, qx, st0, st1, stats, dkv, dkr, dqt, latt, dqn, dqr, wp,
    dkp, sin, acc, zin, fin, hin, xin, xsum, zfin, yin, ys, cin, cs, hi_in, fs, ag,
    q_send, q_recv, kx_send, kx_recv, kz_send, kz_recv, ks_send, ks_recv, l_sem, loc,
    zs_send, zs_recv, kf_send, kf_recv, kf_loc,
    d_send, d_recv, s_send, s_recv, z_send, z_recv, h_send, h_recv, x_send, x_recv, x_loc, zf_send, zf_recv,
    y_send, y_recv, c_send, c_recv, hi_sem, a_send, a_recv,
):
    zh, y, c, x, z = coords()
    s = x // 2
    group = 2 * (x % 2) + c
    sib = device(zh, y, 1 - c, x, z)
    others = [device(zh, y, c, (x + dx) % 4, (z + dz) % 4) for dx in range(4) for dz in range(4) if dx or dz]
    others += [device(zh, y, 1 - c, (x + d) % 4, z) for d in range(4)]
    others += [device(zh, (y + d) % 4, cc, x, z) for d in (1, 2, 3) for cc in (0, 1)]
    others += [device(1 - zh, y, c, x, z)]
    lane = lax.broadcasted_iota(jnp.int32, (1, 2 * ROPE), 1)

    def rows(at, size=BLOCK):
        return pl.ds(pl.multiple_of(at * BLOCK, BLOCK), size)

    def wide_rows(p):
        return pl.ds(pl.multiple_of(p * WIDE, WIDE), WIDE)

    w_copy = pltpu.make_async_copy(kv_up.at[:, pl.ds(pl.multiple_of(group * 1024, 1024), 1024)], w, loc.at[4])
    w_copy.start()
    kblk[:, 0:LATENT] = lat[...]
    pair = krope[...].T
    own_lens[...] = jnp.zeros(own_lens.shape, jnp.int32)
    own_lens[0:1, 0:8] = lens[...]
    kblk[:, LATENT:KEYS] = jnp.concatenate([pair, pair], axis=1)
    greet(others)

    def key_send(t):
        return remote(kblk, keys.at[rows(x)], kx_send.at[t], kx_recv.at[x // 2], device(zh, y, x % 2, 2 * c + t, z))

    def key_local():
        return pltpu.make_async_copy(kblk, keys.at[rows(x)], loc.at[0])

    key_self = [(2 * c + t == x) & (x % 2 == c) for t in (0, 1)]
    for t in (0, 1):
        @pl.when(jnp.logical_not(key_self[t]))
        def _():
            key_send(t).start()

        @pl.when(key_self[t])
        def _():
            key_local().start()

    def zs_copy(p):
        return remote(
            kblk.at[HALF:BLOCK], zstage.at[p - 1], zs_send.at[p - 1], zs_recv.at[p - 1], device(zh, y, c, x, across(z, p))
        )

    for p in (1, 2, 3):
        zs_copy(p).start()

    def q_copies(g, target):
        wide = pl.ds(g * GROUP * DIM, GROUP * DIM)
        thin = pl.ds(g * GROUP * ROPE, GROUP * ROPE)
        return [
            remote(nope.at[:, wide], qn.at[rows(x)], q_send.at[0, g], q_recv.at[0, x], target),
            remote(rope.at[:, thin], qr.at[rows(x)], q_send.at[2, g], q_recv.at[2, x], target),
            remote(gout.at[:, wide], go.at[rows(x)], q_send.at[1, g], q_recv.at[1, x], target),
        ]

    def q_local(g):
        wide = pl.ds(g * GROUP * DIM, GROUP * DIM)
        thin = pl.ds(g * GROUP * ROPE, GROUP * ROPE)
        return [
            pltpu.make_async_copy(nope.at[:, wide], qn.at[rows(x)], loc.at[1]),
            pltpu.make_async_copy(gout.at[:, wide], go.at[rows(x)], loc.at[2]),
            pltpu.make_async_copy(rope.at[:, thin], qr.at[rows(x)], loc.at[3]),
        ]

    q_self = [(2 * c + g // 2 == x) & (c == g % 2) for g in range(4)]
    for g in range(4):
        @pl.when(jnp.logical_not(q_self[g]))
        def _():
            for copy in q_copies(g, device(zh, y, g % 2, 2 * c + g // 2, z)):
                copy.start()

        @pl.when(q_self[g])
        def _():
            for copy in q_local(g):
                copy.start()

    lens_copy = remote(own_lens, other_lens, l_sem.at[0], l_sem.at[1], sib)
    lens_copy.start()

    def key_rows(p, k, core):
        return rows(4 * p + core + 2 * k)

    def half_rows(p, k, core, half):
        return pl.ds(pl.multiple_of((4 * p + core + 2 * k) * BLOCK + half * HALF, HALF), HALF)

    def z_key(k, p):
        return remote(
            keys.at[half_rows(0, k, c, 0)], keys.at[half_rows(p, k, c, 0)],
            kz_send.at[k, p - 1], kz_recv.at[k, p - 1], device(zh, y, c, x, across(z, p)),
        )

    def kf_copy(t, p):
        return remote(
            zstage.at[p - 1], keys.at[half_rows(p, x // 2, x % 2, 1)],
            kf_send.at[t, p - 1], kf_recv.at[x // 2, p - 1], device(zh, y, x % 2, 2 * c + t, z),
        )

    def kf_local(p):
        return pltpu.make_async_copy(zstage.at[p - 1], keys.at[half_rows(p, x // 2, x % 2, 1)], kf_loc.at[p - 1])

    def sib_key(k, p, core):
        at = key_rows(p, k, core)
        return remote(keys.at[at], keys.at[at], ks_send.at[k, p], ks_recv.at[k, p], sib)

    for k in (0, 1):
        own = c + 2 * k
        self_here = (own == x) & (s == c)

        @pl.when(jnp.logical_not(self_here))
        def _():
            remote(kblk, keys.at[rows(own)], kx_send.at[0], kx_recv.at[k], sib).wait_recv()

        @pl.when(self_here)
        def _():
            key_local().wait()

        for p in (1, 2, 3):
            z_key(k, p).start()
        sib_key(k, 0, c).start()

    def take(p):
        for k in (0, 1):
            sib_key(k, p, 1 - c).wait_recv()

    def pass_on(p):
        for k in (0, 1):
            z_key(k, p).wait_recv()
            self_here = (c + 2 * k == x) & (s == c)

            @pl.when(jnp.logical_not(self_here))
            def _():
                remote(zstage.at[p - 1], keys.at[half_rows(p, k, c, 1)], kf_send.at[0, p - 1], kf_recv.at[k, p - 1], sib).wait_recv()

            @pl.when(self_here)
            def _():
                kf_local(p).wait()

            sib_key(k, p, c).start()

    w_copy.wait()
    wt = [w[:, h * 256:h * 256 + DIM].T for h in range(GROUP)]

    def project(p):
        at = wide_rows(p)
        own = keys[at, 0:LATENT]
        rot = keys[at, LATENT:KEYS]
        rot_t = rot.T
        for h in range(GROUP):
            both = dot(own, w[:, h * 256:(h + 1) * 256]).astype(BF16)
            kx[at, h * 256:h * 256 + DIM] = both[:, 0:DIM]
            kx[at, h * 256 + DIM:(h + 1) * 256] = rot
            vx[at, h * DIM:(h + 1) * DIM] = both[:, DIM:256]
            ktx[h, 0:DIM, at] = dot_bt(wt[h], own).astype(BF16)
            ktx[h, DIM:256, at] = rot_t
        latt[:, at] = own.T

    take(0)
    project(0)
    for p in (1, 2, 3):
        zs_copy(p).wait_recv()
        for t in (0, 1):
            @pl.when(jnp.logical_not(key_self[t]))
            def _():
                kf_copy(t, p).start()

            @pl.when(key_self[t])
            def _():
                kf_local(p).start()

    lens_copy.wait_recv()
    sizes = jnp.where(s == c, own_lens[0:1, :], other_lens[0:1, :])
    row_lane = lax.broadcasted_iota(jnp.int32, (1, PAIR), 1)
    positions, starts = [], []
    for t in (0, 1):
        pos = (4 * (2 * t + row_lane // BLOCK) + z) * BLOCK + row_lane % BLOCK
        start = jnp.zeros_like(pos)
        end = jnp.zeros_like(sizes[:, 0:1])
        for d in range(8):
            end = end + sizes[:, d:d + 1]
            start = jnp.maximum(start, jnp.where(end <= pos, end, 0))
        positions.append(pos)
        starts.append(start)
    stats[...] = jnp.zeros(stats.shape, F32)
    for h in range(GROUP):
        for t in (0, 1):
            stats[h, t, 0] = jnp.full((8, PAIR), NEGATIVE, F32)
    dqt[...] = jnp.zeros(dqt.shape, F32)

    for xs in range(4):
        self_here = (xs == x) & (s == c)

        @pl.when(jnp.logical_not(self_here))
        def _():
            at = rows(xs)
            remote(nope.at[:, 0:GROUP * DIM], qn.at[at], q_send.at[0, 0], q_recv.at[0, xs], sib).wait_recv()
            remote(rope.at[:, 0:GROUP * ROPE], qr.at[at], q_send.at[2, 0], q_recv.at[2, xs], sib).wait_recv()
            remote(gout.at[:, 0:GROUP * DIM], go.at[at], q_send.at[1, 0], q_recv.at[1, xs], sib).wait_recv()
    for g in range(4):
        @pl.when(q_self[g])
        def _():
            for copy in q_local(g):
                copy.wait()
    for h in range(GROUP):
        qx[:, h * 256:h * 256 + DIM] = qn[:, h * DIM:(h + 1) * DIM]
        half = qr[:, (h // 2) * 128:(h // 2) * 128 + 128]
        keep = (lane < ROPE) if h % 2 == 0 else (lane >= ROPE)
        qx[:, h * 256 + DIM:(h + 1) * 256] = jnp.where(keep, half, jnp.zeros_like(half))

    pairs = [slice(0, PAIR), slice(PAIR, WIDE)]
    spans = [PAIR, WIDE]
    scores = [st0, st1]

    def span(p, t):
        return pl.ds(pl.multiple_of(p * spans[t], spans[t]), spans[t])

    def key_span(p, t):
        return pl.ds(pl.multiple_of(p * WIDE, WIDE), spans[t])

    def look(p):
        base = lax.broadcasted_iota(jnp.int32, (WIDE, 1), 0)
        key = base + (base // BLOCK) * (3 * BLOCK) + across(z, p) * BLOCK
        for t in (0, 1):
            part = key[0:spans[t]]
            seen = (part <= positions[t]) & (part >= starts[t])
            for h in range(GROUP):
                at = key_span(p, t)
                v = dot_bt(kx[at, h * 256:(h + 1) * 256], qx[pairs[t], h * 256:(h + 1) * 256])
                d = dot_bt(vx[at, h * DIM:(h + 1) * DIM], go[pairs[t], h * DIM:(h + 1) * DIM])
                v = jnp.where(seen, v * (SCALE * math.log2(math.e)), NEGATIVE)
                scores[t][h, span(p, t), :] = v
                old = stats[h, t, 0]
                top = jnp.maximum(old, fold(v, jnp.max))
                e = jnp.exp2(v.reshape(spans[t] // 8, 8, PAIR) - top[None])
                factor = jnp.exp2(old - top)
                stats[h, t, 0] = top
                stats[h, t, 1] = stats[h, t, 1] * factor + jnp.sum(e, axis=0)
                stats[h, t, 2] = stats[h, t, 2] * factor + jnp.sum(e * d.reshape(spans[t] // 8, 8, PAIR), axis=0)

    look(0)

    def arrive(p, carry):
        pass_on(p)
        take(p)
        project(p)
        look(p)
        return carry

    lax.fori_loop(1, 4, arrive, 0)

    logs, inners = [], []
    for h in range(GROUP):
        for t in (0, 1):
            top8 = stats[h, t, 0]
            top = jnp.max(top8, axis=0, keepdims=True)
            factor = jnp.exp2(top8 - top)
            total = jnp.sum(stats[h, t, 1] * factor, axis=0, keepdims=True)
            inners.append(jnp.sum(stats[h, t, 2] * factor, axis=0, keepdims=True) / total)
            logs.append(top + jnp.log2(total))

    def grads(p):
        at = wide_rows(p)
        low = pl.ds(pl.multiple_of(p * WIDE, WIDE), PAIR)
        high = pl.ds(pl.multiple_of(p * WIDE + PAIR, PAIR), PAIR)
        rot_low = jnp.zeros((PAIR, 2 * ROPE), F32)
        rot_high = jnp.zeros((PAIR, 2 * ROPE), F32)
        for h in range(GROUP):
            probs, diffs = [], []
            for t in (0, 1):
                e = jnp.exp2(scores[t][h, span(p, t), :] - logs[2 * h + t])
                d = dot_bt(vx[key_span(p, t), h * DIM:(h + 1) * DIM], go[pairs[t], h * DIM:(h + 1) * DIM])
                diff = (e * (d - inners[2 * h + t])).astype(BF16)
                dqt[h, t] += dot(ktx[h, :, key_span(p, t)], diff)
                probs.append(e.astype(BF16))
                diffs.append(diff)
            q_at, g_at = slice(h * 256, (h + 1) * 256), slice(h * DIM, (h + 1) * DIM)
            dk = SCALE * dot(jnp.concatenate([diffs[0], diffs[1][0:PAIR]], axis=1), qx[:, q_at])
            dv = dot(jnp.concatenate([probs[0], probs[1][0:PAIR]], axis=1), go[:, g_at])
            dkv[low, h * 256:h * 256 + DIM] = dk[:, 0:DIM].astype(BF16)
            dkv[low, h * 256 + DIM:(h + 1) * 256] = dv.astype(BF16)
            rot_low = rot_low + dk[:, DIM:256]
            dk = SCALE * dot(diffs[1][PAIR:WIDE], qx[pairs[1], q_at])
            dv = dot(probs[1][PAIR:WIDE], go[pairs[1], g_at])
            dkv[high, h * 256:h * 256 + DIM] = dk[:, 0:DIM].astype(BF16)
            dkv[high, h * 256 + DIM:(h + 1) * 256] = dv.astype(BF16)
            rot_high = rot_high + dk[:, DIM:256]
        dkr[low, :] = rot_low
        dkr[high, :] = rot_high

    def d_places():
        wide = pl.ds(pl.multiple_of(group * 512, 512), 512)
        thin = pl.ds(pl.multiple_of(group * 256, 256), 256)
        return o_qn.at[:, wide], o_qr.at[:, thin]

    def d_copies(xs):
        target = device(zh, y, s, xs, z)
        at = rows(xs)
        wide, thin = d_places()
        return [
            remote(dqn.at[at], wide, d_send.at[0, xs], d_recv.at[0, group], target),
            remote(dqr.at[at], thin, d_send.at[1, xs], d_recv.at[1, group], target),
        ]

    def d_local():
        at = rows(x)
        wide, thin = d_places()
        return [
            pltpu.make_async_copy(dqn.at[at], wide, loc.at[5]),
            pltpu.make_async_copy(dqr.at[at], thin, loc.at[6]),
        ]

    d_self = [(xs == x) & (s == c) for xs in range(4)]

    def send_queries():
        for t in (0, 1):
            rots = []
            for h in range(GROUP):
                dq = SCALE * dqt[h, t].T
                dqn[pairs[t], h * DIM:(h + 1) * DIM] = dq[:, 0:DIM].astype(BF16)
                rots.append(dq[:, DIM:256])
            for half in (0, 1):
                both = jnp.where(lane < ROPE, rots[2 * half], rots[2 * half + 1])
                dqr[pairs[t], half * 128:(half + 1) * 128] = both.astype(BF16)
        for xs in range(4):
            @pl.when(jnp.logical_not(d_self[xs]))
            def _():
                for copy in d_copies(xs):
                    copy.start()

            @pl.when(d_self[xs])
            def _():
                for copy in d_local():
                    copy.start()

    def y_copy(d):
        peer = (y + d) % 4
        return remote(
            wp.at[:, pl.ds(pl.multiple_of(peer * 256, 256), 256)], yin.at[d - 1],
            y_send.at[d - 1], y_recv.at[d - 1], device(zh, peer, c, x, z),
        )

    def send_weights():
        for n in range(GROUP):
            wp[:, n * 256:(n + 1) * 256] = dot(latt[...], dkv[:, n * 256:(n + 1) * 256]).astype(BF16)
        for d in (2, 1, 3):
            y_copy(d).start()

    def s_copy(k, p):
        return remote(dkp.at[key_rows(p, k, 1 - c)], sin.at[p, k], s_send.at[k, p], s_recv.at[k, p], sib)

    def z_copy(k, p):
        return remote(
            acc.at[p, k, pl.ds(0, HALF)], zin.at[p - 1, k],
            z_send.at[k, p - 1], z_recv.at[k, p - 1], device(zh, y, c, x, across(z, p)),
        )

    def x_copy(k, p):
        return remote(
            acc.at[p, k, pl.ds(HALF, HALF)], xin.at[p, x % 2],
            x_send.at[k, p], x_recv.at[x % 2, p], device(zh, y, s, c + 2 * k, z),
        )

    def x_local(k, p):
        return pltpu.make_async_copy(acc.at[p, k, pl.ds(HALF, HALF)], xin.at[p, x % 2], x_loc.at[p])

    h_self = [(c + 2 * k == x) & (s == c) for k in (0, 1)]

    def join(p):
        for k in (0, 1):
            s_copy(k, p).wait_recv()
            acc[p, k] = (dkp[key_rows(p, k, c), :].astype(F32) + sin[p, k].astype(F32)).astype(BF16)

            @pl.when(jnp.logical_not(h_self[k]))
            def _():
                x_copy(k, p).start()

            @pl.when(h_self[k])
            def _():
                x_local(k, p).start()

    def back(q, carry):
        p = 3 - q
        grads(p)
        at = wide_rows(p)
        dkp[at, 0:LATENT] = dot_bt(dkv[at, :], w[...]).astype(BF16)
        rot = dkr[at, :]
        dkp[at, LATENT:KEYS] = (rot + pltpu.roll(rot, ROPE, 1)).astype(BF16)
        for k in (0, 1):
            s_copy(k, p).start()

        @pl.when(q > 0)
        def _():
            join(p + 1)
            for k in (0, 1):
                z_copy(k, p + 1).start()
        return carry

    lax.fori_loop(0, 4, back, 0)
    send_weights()
    send_queries()
    join(0)

    def zf_copy(p):
        return remote(xsum.at[p - 1], zfin.at[p - 1], zf_send.at[p - 1], zf_recv.at[p - 1], device(zh, y, c, x, across(z, p)))

    def x_total(p):
        for t in (0, 1):
            self_here = (2 * c + t == x) & (x % 2 == c)

            @pl.when(jnp.logical_not(self_here))
            def _():
                remote(acc.at[p, 0, pl.ds(HALF, HALF)], xin.at[p, t], x_send.at[0, p], x_recv.at[t, p], sib).wait_recv()

            @pl.when(self_here)
            def _():
                x_local(0, p).wait()
        return xin[p, 0].astype(F32) + xin[p, 1].astype(F32)

    for p in (3, 2, 1):
        xsum[p - 1] = x_total(p).astype(BF16)
        zf_copy(p).start()
    second = x_total(0)

    for d in (1, 3, 2):
        y_copy(d).wait_recv()
    mine = wp[:, pl.ds(pl.multiple_of(y * 256, 256), 256)].astype(F32)
    ys[...] = (mine + yin[0].astype(F32) + yin[1].astype(F32) + yin[2].astype(F32)).astype(BF16)

    def c_copy(dx, dz):
        px, pz = (x + dx) % 4, (z + dz) % 4
        src = ys.at[pl.ds(pl.multiple_of((4 * px + pz) * 32, 32), 32)]
        return remote(src, cin.at[dx, dz], c_send.at[dx, dz], c_recv.at[dx, dz], device(zh, y, c, px, pz))

    mates = [(dx, dz) for dz in (2, 1, 3, 0) for dx in (2, 1, 3, 0) if dx or dz]
    for dx, dz in mates:
        c_copy(dx, dz).start()

    def h_copy(k):
        return remote(fin.at[k], hin.at[x % 2], h_send.at[k], h_recv.at[x % 2], device(zh, y, s, c + 2 * k, z))

    def h_local(k):
        return pltpu.make_async_copy(fin.at[k], hin.at[x % 2], loc.at[7])

    for k in (0, 1):
        total = acc[0, k, 0:HALF, :].astype(F32)
        for p in (3, 2, 1):
            z_copy(k, p).wait_recv()
            total = total + zin[p - 1, k].astype(F32)
        fin[k] = total.astype(BF16)

        @pl.when(jnp.logical_not(h_self[k]))
        def _():
            h_copy(k).start()

        @pl.when(h_self[k])
        def _():
            h_local(k).start()

    for dx, dz in mates:
        c_copy(dx, dz).wait_recv()
    own = ys[pl.ds(pl.multiple_of((4 * x + z) * 32, 32), 32), :].astype(F32)
    even = own
    for dz in (1, 2, 3):
        even = even + cin[0, dz].astype(F32)
    for dz in range(4):
        even = even + cin[2, dz].astype(F32)
    odd = jnp.zeros_like(own)
    for dx in (1, 3):
        for dz in range(4):
            odd = odd + cin[dx, dz].astype(F32)
    flip = x % 2 == 1
    cs[:, 0:256] = jnp.where(flip, odd, even).astype(BF16)
    cs[:, 256:512] = jnp.where(flip, even, odd).astype(BF16)
    hi_copy = remote(cs, hi_in, hi_sem.at[0], hi_sem.at[1], device(1 - zh, y, c, x, z))
    hi_copy.start()

    for t in (0, 1):
        self_here = (2 * c + t == x) & (x % 2 == c)

        @pl.when(jnp.logical_not(self_here))
        def _():
            remote(fin.at[0], hin.at[t], h_send.at[0], h_recv.at[t], sib).wait_recv()
    for k in (0, 1):
        @pl.when(h_self[k])
        def _():
            h_local(k).wait()
    for p in (1, 2, 3):
        zf_copy(p).wait_recv()
        second = second + zfin[p - 1].astype(F32)
    final = jnp.concatenate([hin[0].astype(F32) + hin[1].astype(F32), second], axis=0)
    o_lat[...] = final[:, 0:LATENT].astype(BF16)
    o_rot[...] = final[:, LATENT:KEYS].T[0:ROPE, :].astype(BF16)

    hi_copy.wait_recv()
    fs[...] = (cs[...].astype(F32) + hi_in[...].astype(F32)).astype(BF16)

    def a_copy(dy, dc):
        peer = device(zh, (y + dy) % 4, (c + dc) % 2, x, z)
        return remote(fs, ag.at[dy, dc], a_send.at[dy, dc], a_recv.at[dy, dc], peer)

    members = [(dy, dc) for dy in (2, 1, 3, 0) for dc in (0, 1) if dy or dc]
    for dy, dc in members:
        a_copy(dy, dc).start()

    def place(values, from_y, from_c):
        wide = values.astype(F32)
        for parity in (0, 1):
            at = pl.multiple_of((2 * parity + from_c) * 1024 + from_y * 256, 256)
            o_w[:, pl.ds(at, 256)] = wide[:, parity * 256:(parity + 1) * 256]

    place(fs[...], y, c)
    for dy, dc in members:
        a_copy(dy, dc).wait_recv()
        place(ag[dy, dc], (y + 4 - dy) % 4, (c + dc) % 2)

    for gs in range(4):
        self_here = (group == gs) & (s == c)

        @pl.when(jnp.logical_not(self_here))
        def _():
            remote(dqn.at[0:BLOCK], o_qn.at[:, gs * 512:(gs + 1) * 512], d_send.at[0, 0], d_recv.at[0, gs], sib).wait_recv()
            remote(dqr.at[0:BLOCK], o_qr.at[:, gs * 256:(gs + 1) * 256], d_send.at[1, 0], d_recv.at[1, gs], sib).wait_recv()

    for t in (0, 1):
        @pl.when(jnp.logical_not(key_self[t]))
        def _():
            key_send(t).wait_send()
    for g in range(4):
        @pl.when(jnp.logical_not(q_self[g]))
        def _():
            for copy in q_copies(g, sib):
                copy.wait_send()
    lens_copy.wait_send()
    for k in (0, 1):
        for p in (1, 2, 3):
            z_key(k, p).wait_send()
            z_copy(k, p).wait_send()
        for p in range(4):
            sib_key(k, p, c).wait_send()
            s_copy(k, p).wait_send()

        @pl.when(jnp.logical_not(h_self[k]))
        def _():
            h_copy(k).wait_send()
    for p in (1, 2, 3):
        zs_copy(p).wait_send()
        zf_copy(p).wait_send()
        for t in (0, 1):
            @pl.when(jnp.logical_not(key_self[t]))
            def _():
                kf_copy(t, p).wait_send()
    for k in (0, 1):
        for p in range(4):
            @pl.when(jnp.logical_not(h_self[k]))
            def _():
                x_copy(k, p).wait_send()
    for xs in range(4):
        @pl.when(jnp.logical_not(d_self[xs]))
        def _():
            for copy in d_copies(xs):
                copy.wait_send()

        @pl.when(d_self[xs])
        def _():
            for copy in d_local():
                copy.wait()
    for d in (1, 2, 3):
        y_copy(d).wait_send()
    for dx, dz in mates:
        c_copy(dx, dz).wait_send()
    hi_copy.wait_send()
    for dy, dc in members:
        a_copy(dy, dc).wait_send()


def shape(dims, kind=BF16):
    return jax.ShapeDtypeStruct(dims, kind)


def dma(*dims):
    return pltpu.SemaphoreType.DMA(dims)


def finish_kernel(*refs):
    sems = refs[15]
    into = [pltpu.make_async_copy(refs[i], refs[10 + i], sems.at[0, i]) for i in range(5)]
    out = [pltpu.make_async_copy(refs[10 + i], refs[5 + i], sems.at[1, i]) for i in range(5)]
    for copy in into:
        copy.start()
    for i in range(5):
        into[i].wait()
        out[i].start()
    for copy in out:
        copy.wait()


def body(query_nope, query_rope, latent, key_rope, grad_output, kv_up, doc_lengths):
    here = pl.BlockSpec(memory_space=pltpu.VMEM)
    outs = pl.pallas_call(
        kernel,
        name="whole_rows",
        out_shape=(
            shape((BLOCK, HEADS * DIM)),
            shape((BLOCK, HEADS * ROPE)),
            shape((BLOCK, LATENT)),
            shape((ROPE, BLOCK)),
            shape((32, HEADS * 256), F32),
        ),
        in_specs=[here] * 6 + [pl.BlockSpec(memory_space=pl.ANY)],
        out_specs=(here,) * 5,
        scratch_shapes=[
            VMEM((BLOCK, KEYS), BF16),
            VMEM((LATENT, GROUP * 256), BF16),
            VMEM((WIDE, GROUP * DIM), BF16),
            VMEM((WIDE, GROUP * DIM), BF16),
            VMEM((WIDE, GROUP * ROPE), BF16),
            VMEM((8, 128), jnp.int32),
            VMEM((8, 128), jnp.int32),
            VMEM((SEQ, KEYS), BF16),
            VMEM((3, HALF, KEYS), BF16),
            VMEM((SEQ, GROUP * 256), BF16),
            VMEM((SEQ, GROUP * DIM), BF16),
            VMEM((GROUP, 256, SEQ), BF16),
            VMEM((WIDE, GROUP * 256), BF16),
            VMEM((GROUP, 4 * PAIR, PAIR), F32),
            VMEM((GROUP, 4 * WIDE, PAIR), F32),
            VMEM((GROUP, 2, 3, 8, PAIR), F32),
            VMEM((SEQ, GROUP * 256), BF16),
            VMEM((SEQ, 128), F32),
            VMEM((GROUP, 2, 256, PAIR), F32),
            VMEM((LATENT, SEQ), BF16),
            VMEM((WIDE, GROUP * DIM), BF16),
            VMEM((WIDE, GROUP * ROPE), BF16),
            VMEM((LATENT, GROUP * 256), BF16),
            VMEM((SEQ, KEYS), BF16),
            VMEM((4, 2, BLOCK, KEYS), BF16),
            VMEM((4, 2, BLOCK, KEYS), BF16),
            VMEM((3, 2, HALF, KEYS), BF16),
            VMEM((2, HALF, KEYS), BF16),
            VMEM((2, HALF, KEYS), BF16),
            VMEM((4, 2, HALF, KEYS), BF16),
            VMEM((3, HALF, KEYS), BF16),
            VMEM((3, HALF, KEYS), BF16),
            VMEM((3, LATENT, 256), BF16),
            VMEM((LATENT, 256), BF16),
            VMEM((4, 4, 32, 256), BF16),
            VMEM((32, 512), BF16),
            VMEM((32, 512), BF16),
            VMEM((32, 512), BF16),
            VMEM((4, 2, 32, 512), BF16),
            dma(3, 4), dma(3, 4), dma(2), dma(2), dma(2, 3), dma(2, 3), dma(2, 4), dma(2, 4), dma(2), dma(8),
            dma(3), dma(3), dma(2, 3), dma(2, 3), dma(3),
            dma(2, 4), dma(2, 4), dma(2, 4), dma(2, 4), dma(2, 3), dma(2, 3), dma(2), dma(2),
            dma(2, 4), dma(2, 4), dma(4), dma(3), dma(3),
            dma(3), dma(3), dma(4, 4), dma(4, 4), dma(2), dma(4, 2), dma(4, 2),
        ],
        compiler_params=pltpu.CompilerParams(collective_id=0, has_side_effects=True, vmem_limit_bytes=58 * MIB),
    )(query_nope[0], query_rope[0], grad_output[0], latent[0], key_rope[0].T, doc_lengths, kv_up)
    anywhere = pl.BlockSpec(memory_space=pl.ANY)
    gqn, gqr, glat, grot, gw = pl.pallas_call(
        finish_kernel,
        name="finish_rows",
        out_shape=[shape(out.shape, out.dtype) for out in outs],
        in_specs=[anywhere] * 5,
        out_specs=[anywhere] * 5,
        scratch_shapes=[VMEM(out.shape, out.dtype) for out in outs] + [dma(2, 5)],
    )(*outs)
    return gqn[None], gqr[None], glat[None], grot.T[None], gw


def solution(mesh):
    rows = P("dp", "ctx", None)
    return jax.shard_map(
        body,
        mesh=mesh,
        in_specs=(rows, rows, rows, rows, rows, P(), P("dp", None)),
        out_specs=(rows, rows, rows, rows, P("ctx", None)),
        check_vma=False,
    )
```

time: 149 us -> 98.4 us (0.66)
  Pallas kernels: 127 us -> 97.7 us
  local copies, waits for them, and re-layouts: 20.1 us -> 0 us
    pallas_call x3 -> x2, Pallas kernels: 127 us -> 97.7 us  [the longest x1 95.4 us: body(): pl.pallas_call(kernel, name='whole_rows', out_shape=(shape((BLOCK, HEADS...]
    unnamed x30 -> x0, local copies, waits for them, and re-layouts: 17.1 us -> none
    dynamic_slice x1 -> x0, local copies, waits for them, and re-layouts: 2.32 us -> none  [body(): w = lax.dynamic_slice_in_dim(kv_up, g * GROUP * 256, GROUP * 256, 1)]
where the time goes in v2:
time: 98.4 us; the launch traced here: 98.3 us
  Pallas kernels  97.7 us (99%)
    pallas_call x1, Pallas kernels, body(): pl.pallas_call(kernel, name='whole_rows', out_shape=(shape((BLOCK, HEADS...  95.4 us
    pallas_call x1, Pallas kernels, body(): pl.pallas_call(finish_kernel, name='finish_rows', out_shape=[shape(out.sh...  2.23 us

profile of v2, /device:TPU:1, one launch (start us, length us, event | category | flops | bytes accessed | tf_op | source)
XLA Modules:
  0.0 98.3 jit_solution(8541440247155933168)
XLA Ops:
  0.6 95.4 %whole_rows.1 = (bf16[128,2048]{1,0:T(8,128)(2,1)}, bf16[128,1024]{1,0:T(8,128)(2,1)}, bf16[128,512]{1,0:T(8,128)(2,1)}, bf16[64,128]{1,0:T(8,128)(2,1)}, f32[32,4096]{1,0:T(8,128)}) custom-call(bf16[128,2048]{1,0:T(8,128)(2,1)} %bitcast.13, bf16[128,1024]{1,0:T(8,128)(2,1)} %bitcast.15, bf16[128,2048]{1,0:T(8,128)(2,1)} %bitcast.14, ...), custom_call_target="tpu_custom_call" | custom-call | tf_op jit(solution)/shard_map/whole_rows/pallas_call | solution.py:682
  96.1 2.2 %finish_rows.1 = (bf16[128,2048]{1,0:T(8,128)(2,1)}, bf16[128,1024]{1,0:T(8,128)(2,1)}, bf16[128,512]{1,0:T(8,128)(2,1)}, bf16[64,128]{1,0:T(8,128)(2,1)}, f32[32,4096]{1,0:T(8,128)}) custom-call(bf16[128,2048]{1,0:T(8,128)(2,1)} %get-tuple-element.15.refs_0_, bf16[128,1024]{1,0:T(8,128)(2,1)} %get-tuple-element.16.refs_1_, ...), custom_call_target="tpu_custom_call" | custom-call | tf_op jit(solution)/shard_map/finish_rows/pallas_call | solution.py:743

commit v3 on v2

--- a/solution.py
+++ b/solution.py
@@ -56,7 +56,6 @@
 
 PAIR = 2 * BLOCK
 WIDE = 4 * BLOCK
-HALF = BLOCK // 2
 KEYS = LATENT + 2 * ROPE
 
 
@@ -75,7 +74,7 @@
     kx, vx, ktx, qx, st0, st1, stats, dkv, dkr, dqt, latt, dqn, dqr, wp,
     dkp, sin, acc, zin, fin, hin, xin, xsum, zfin, yin, ys, cin, cs, hi_in, fs, ag,
     q_send, q_recv, kx_send, kx_recv, kz_send, kz_recv, ks_send, ks_recv, l_sem, loc,
-    zs_send, zs_recv, kf_send, kf_recv, kf_loc,
+    zs_sem, kf_send, kf_recv,
     d_send, d_recv, s_send, s_recv, z_send, z_recv, h_send, h_recv, x_send, x_recv, x_loc, zf_send, zf_recv,
     y_send, y_recv, c_send, c_recv, hi_sem, a_send, a_recv,
 ):
@@ -120,13 +119,10 @@
         def _():
             key_local().start()
 
-    def zs_copy(p):
-        return remote(
-            kblk.at[HALF:BLOCK], zstage.at[p - 1], zs_send.at[p - 1], zs_recv.at[p - 1], device(zh, y, c, x, across(z, p))
-        )
-
-    for p in (1, 2, 3):
-        zs_copy(p).start()
+    def zs_copy():
+        return remote(kblk, zstage, zs_sem.at[0], zs_sem.at[1], device(zh, y, c, x, across(z, 3)))
+
+    zs_copy().start()
 
     def q_copies(g, target):
         wide = pl.ds(g * GROUP * DIM, GROUP * DIM)
@@ -164,23 +160,20 @@
     def key_rows(p, k, core):
         return rows(4 * p + core + 2 * k)
 
-    def half_rows(p, k, core, half):
-        return pl.ds(pl.multiple_of((4 * p + core + 2 * k) * BLOCK + half * HALF, HALF), HALF)
-
     def z_key(k, p):
         return remote(
-            keys.at[half_rows(0, k, c, 0)], keys.at[half_rows(p, k, c, 0)],
+            keys.at[key_rows(0, k, c)], keys.at[key_rows(p, k, c)],
             kz_send.at[k, p - 1], kz_recv.at[k, p - 1], device(zh, y, c, x, across(z, p)),
         )
 
-    def kf_copy(t, p):
+    def kf_copy(t):
         return remote(
-            zstage.at[p - 1], keys.at[half_rows(p, x // 2, x % 2, 1)],
-            kf_send.at[t, p - 1], kf_recv.at[x // 2, p - 1], device(zh, y, x % 2, 2 * c + t, z),
+            zstage, keys.at[key_rows(3, x // 2, x % 2)],
+            kf_send.at[t], kf_recv.at[x // 2], device(zh, y, x % 2, 2 * c + t, z),
         )
 
-    def kf_local(p):
-        return pltpu.make_async_copy(zstage.at[p - 1], keys.at[half_rows(p, x // 2, x % 2, 1)], kf_loc.at[p - 1])
+    def kf_local():
+        return pltpu.make_async_copy(zstage, keys.at[key_rows(3, x // 2, x % 2)], loc.at[0])
 
     def sib_key(k, p, core):
         at = key_rows(p, k, core)
@@ -198,7 +191,7 @@
         def _():
             key_local().wait()
 
-        for p in (1, 2, 3):
+        for p in (1, 2):
             z_key(k, p).start()
         sib_key(k, 0, c).start()
 
@@ -209,17 +202,21 @@
     def pass_on(p):
         for k in (0, 1):
             z_key(k, p).wait_recv()
+            sib_key(k, p, c).start()
+
+    def pass_last():
+        for k in (0, 1):
             self_here = (c + 2 * k == x) & (s == c)
 
             @pl.when(jnp.logical_not(self_here))
             def _():
-                remote(zstage.at[p - 1], keys.at[half_rows(p, k, c, 1)], kf_send.at[0, p - 1], kf_recv.at[k, p - 1], sib).wait_recv()
+                remote(zstage, keys.at[key_rows(3, k, c)], kf_send.at[0], kf_recv.at[k], sib).wait_recv()
 
             @pl.when(self_here)
             def _():
-                kf_local(p).wait()
-
-            sib_key(k, p, c).start()
+                kf_local().wait()
+
+            sib_key(k, 3, c).start()
 
     w_copy.wait()
     wt = [w[:, h * 256:h * 256 + DIM].T for h in range(GROUP)]
@@ -238,18 +235,25 @@
             ktx[h, DIM:256, at] = rot_t
         latt[:, at] = own.T
 
-    take(0)
-    project(0)
-    for p in (1, 2, 3):
-        zs_copy(p).wait_recv()
-        for t in (0, 1):
-            @pl.when(jnp.logical_not(key_self[t]))
-            def _():
-                kf_copy(t, p).start()
-
-            @pl.when(key_self[t])
-            def _():
-                kf_local(p).start()
+    def first(p, carry):
+        @pl.when(p == 1)
+        def _():
+            zs_copy().wait_recv()
+            for t in (0, 1):
+                @pl.when(jnp.logical_not(key_self[t]))
+                def _():
+                    kf_copy(t).start()
+
+                @pl.when(key_self[t])
+                def _():
+                    kf_local().start()
+            pass_on(1)
+
+        take(p)
+        project(p)
+        return carry
+
+    lax.fori_loop(0, 2, first, 0)
 
     lens_copy.wait_recv()
     sizes = jnp.where(s == c, own_lens[0:1, :], other_lens[0:1, :])
@@ -320,16 +324,28 @@
                 stats[h, t, 1] = stats[h, t, 1] * factor + jnp.sum(e, axis=0)
                 stats[h, t, 2] = stats[h, t, 2] * factor + jnp.sum(e * d.reshape(spans[t] // 8, 8, PAIR), axis=0)
 
-    look(0)
-
-    def arrive(p, carry):
-        pass_on(p)
+    def early(p, carry):
+        look(p)
+
+        @pl.when(p == 0)
+        def _():
+            pass_on(2)
+
+        return carry
+
+    def late(p, carry):
         take(p)
         project(p)
+
+        @pl.when(p == 2)
+        def _():
+            pass_last()
+
         look(p)
         return carry
 
-    lax.fori_loop(1, 4, arrive, 0)
+    lax.fori_loop(0, 2, early, 0)
+    lax.fori_loop(2, 4, late, 0)
 
     logs, inners = [], []
     for h in range(GROUP):
@@ -425,26 +441,28 @@
     def send_weights():
         for n in range(GROUP):
             wp[:, n * 256:(n + 1) * 256] = dot(latt[...], dkv[:, n * 256:(n + 1) * 256]).astype(BF16)
-        for d in (2, 1, 3):
-            y_copy(d).start()
+
+            @pl.when(y != n)
+            def _():
+                slot = (n + 3 - y) % 4
+                remote(
+                    wp.at[:, pl.ds(n * 256, 256)], yin.at[slot], y_send.at[slot], y_recv.at[slot], device(zh, n, c, x, z)
+                ).start()
 
     def s_copy(k, p):
         return remote(dkp.at[key_rows(p, k, 1 - c)], sin.at[p, k], s_send.at[k, p], s_recv.at[k, p], sib)
 
-    def z_copy(k, p):
-        return remote(
-            acc.at[p, k, pl.ds(0, HALF)], zin.at[p - 1, k],
-            z_send.at[k, p - 1], z_recv.at[k, p - 1], device(zh, y, c, x, across(z, p)),
-        )
+    def z_copy(k):
+        return remote(acc.at[1, k], zin.at[k], z_send.at[k], z_recv.at[k], device(zh, y, c, x, across(z, 1)))
 
     def x_copy(k, p):
         return remote(
-            acc.at[p, k, pl.ds(HALF, HALF)], xin.at[p, x % 2],
-            x_send.at[k, p], x_recv.at[x % 2, p], device(zh, y, s, c + 2 * k, z),
+            acc.at[p, k], xin.at[p - 2, x % 2],
+            x_send.at[k, p - 2], x_recv.at[x % 2, p - 2], device(zh, y, s, c + 2 * k, z),
         )
 
     def x_local(k, p):
-        return pltpu.make_async_copy(acc.at[p, k, pl.ds(HALF, HALF)], xin.at[p, x % 2], x_loc.at[p])
+        return pltpu.make_async_copy(acc.at[p, k], xin.at[p - 2, x % 2], x_loc.at[p - 2])
 
     h_self = [(c + 2 * k == x) & (s == c) for k in (0, 1)]
 
@@ -453,6 +471,8 @@
             s_copy(k, p).wait_recv()
             acc[p, k] = (dkp[key_rows(p, k, c), :].astype(F32) + sin[p, k].astype(F32)).astype(BF16)
 
+    def send_join(p):
+        for k in (0, 1):
             @pl.when(jnp.logical_not(h_self[k]))
             def _():
                 x_copy(k, p).start()
@@ -474,35 +494,39 @@
         @pl.when(q > 0)
         def _():
             join(p + 1)
+
+        @pl.when((q == 1) | (q == 2))
+        def _():
+            send_join(p + 1)
+
+        @pl.when(q == 3)
+        def _():
             for k in (0, 1):
-                z_copy(k, p + 1).start()
+                z_copy(k).start()
         return carry
 
     lax.fori_loop(0, 4, back, 0)
     send_weights()
-    send_queries()
     join(0)
 
     def zf_copy(p):
-        return remote(xsum.at[p - 1], zfin.at[p - 1], zf_send.at[p - 1], zf_recv.at[p - 1], device(zh, y, c, x, across(z, p)))
-
-    def x_total(p):
+        return remote(xsum.at[p - 2], zfin.at[p - 2], zf_send.at[p - 2], zf_recv.at[p - 2], device(zh, y, c, x, across(z, p)))
+
+    for p in (3, 2):
         for t in (0, 1):
             self_here = (2 * c + t == x) & (x % 2 == c)
 
             @pl.when(jnp.logical_not(self_here))
             def _():
-                remote(acc.at[p, 0, pl.ds(HALF, HALF)], xin.at[p, t], x_send.at[0, p], x_recv.at[t, p], sib).wait_recv()
+                remote(acc.at[p, 0], xin.at[p - 2, t], x_send.at[0, p - 2], x_recv.at[t, p - 2], sib).wait_recv()
 
             @pl.when(self_here)
             def _():
                 x_local(0, p).wait()
-        return xin[p, 0].astype(F32) + xin[p, 1].astype(F32)
-
-    for p in (3, 2, 1):
-        xsum[p - 1] = x_total(p).astype(BF16)
+        xsum[p - 2] = (xin[p - 2, 0].astype(F32) + xin[p - 2, 1].astype(F32)).astype(BF16)
         zf_copy(p).start()
-    second = x_total(0)
+
+    send_queries()
 
     for d in (1, 3, 2):
         y_copy(d).wait_recv()
@@ -525,10 +549,8 @@
         return pltpu.make_async_copy(fin.at[k], hin.at[x % 2], loc.at[7])
 
     for k in (0, 1):
-        total = acc[0, k, 0:HALF, :].astype(F32)
-        for p in (3, 2, 1):
-            z_copy(k, p).wait_recv()
-            total = total + zin[p - 1, k].astype(F32)
+        z_copy(k).wait_recv()
+        total = acc[0, k].astype(F32) + zin[k].astype(F32)
         fin[k] = total.astype(BF16)
 
         @pl.when(jnp.logical_not(h_self[k]))
@@ -567,10 +589,10 @@
         @pl.when(h_self[k])
         def _():
             h_local(k).wait()
-    for p in (1, 2, 3):
+    final = hin[0].astype(F32) + hin[1].astype(F32)
+    for p in (3, 2):
         zf_copy(p).wait_recv()
-        second = second + zfin[p - 1].astype(F32)
-    final = jnp.concatenate([hin[0].astype(F32) + hin[1].astype(F32), second], axis=0)
+        final = final + zfin[p - 2].astype(F32)
     o_lat[...] = final[:, 0:LATENT].astype(BF16)
     o_rot[...] = final[:, LATENT:KEYS].T[0:ROPE, :].astype(BF16)
 
@@ -615,9 +637,9 @@
                 copy.wait_send()
     lens_copy.wait_send()
     for k in (0, 1):
-        for p in (1, 2, 3):
+        for p in (1, 2):
             z_key(k, p).wait_send()
-            z_copy(k, p).wait_send()
+        z_copy(k).wait_send()
         for p in range(4):
             sib_key(k, p, c).wait_send()
             s_copy(k, p).wait_send()
@@ -625,15 +647,14 @@
         @pl.when(jnp.logical_not(h_self[k]))
         def _():
             h_copy(k).wait_send()
-    for p in (1, 2, 3):
-        zs_copy(p).wait_send()
+    zs_copy().wait_send()
+    for t in (0, 1):
+        @pl.when(jnp.logical_not(key_self[t]))
+        def _():
+            kf_copy(t).wait_send()
+    for p in (3, 2):
         zf_copy(p).wait_send()
-        for t in (0, 1):
-            @pl.when(jnp.logical_not(key_self[t]))
-            def _():
-                kf_copy(t, p).wait_send()
-    for k in (0, 1):
-        for p in range(4):
+        for k in (0, 1):
             @pl.when(jnp.logical_not(h_self[k]))
             def _():
                 x_copy(k, p).wait_send()
@@ -700,7 +721,7 @@
             VMEM((8, 128), jnp.int32),
             VMEM((8, 128), jnp.int32),
             VMEM((SEQ, KEYS), BF16),
-            VMEM((3, HALF, KEYS), BF16),
+            VMEM((BLOCK, KEYS), BF16),
             VMEM((SEQ, GROUP * 256), BF16),
             VMEM((SEQ, GROUP * DIM), BF16),
             VMEM((GROUP, 256, SEQ), BF16),
@@ -718,24 +739,24 @@
             VMEM((SEQ, KEYS), BF16),
             VMEM((4, 2, BLOCK, KEYS), BF16),
             VMEM((4, 2, BLOCK, KEYS), BF16),
-            VMEM((3, 2, HALF, KEYS), BF16),
-            VMEM((2, HALF, KEYS), BF16),
-            VMEM((2, HALF, KEYS), BF16),
-            VMEM((4, 2, HALF, KEYS), BF16),
-            VMEM((3, HALF, KEYS), BF16),
-            VMEM((3, HALF, KEYS), BF16),
-            VMEM((3, LATENT, 256), BF16),
+            VMEM((2, BLOCK, KEYS), BF16),
+            VMEM((2, BLOCK, KEYS), BF16),
+            VMEM((2, BLOCK, KEYS), BF16),
+            VMEM((2, 2, BLOCK, KEYS), BF16),
+            VMEM((2, BLOCK, KEYS), BF16),
+            VMEM((2, BLOCK, KEYS), BF16),
+            VMEM((4, LATENT, 256), BF16),
             VMEM((LATENT, 256), BF16),
             VMEM((4, 4, 32, 256), BF16),
             VMEM((32, 512), BF16),
             VMEM((32, 512), BF16),
             VMEM((32, 512), BF16),
             VMEM((4, 2, 32, 512), BF16),
-            dma(3, 4), dma(3, 4), dma(2), dma(2), dma(2, 3), dma(2, 3), dma(2, 4), dma(2, 4), dma(2), dma(8),
-            dma(3), dma(3), dma(2, 3), dma(2, 3), dma(3),
-            dma(2, 4), dma(2, 4), dma(2, 4), dma(2, 4), dma(2, 3), dma(2, 3), dma(2), dma(2),
-            dma(2, 4), dma(2, 4), dma(4), dma(3), dma(3),
-            dma(3), dma(3), dma(4, 4), dma(4, 4), dma(2), dma(4, 2), dma(4, 2),
+            dma(3, 4), dma(3, 4), dma(2), dma(2), dma(2, 2), dma(2, 2), dma(2, 4), dma(2, 4), dma(2), dma(8),
+            dma(2), dma(2), dma(2),
+            dma(2, 4), dma(2, 4), dma(2, 4), dma(2, 4), dma(2), dma(2), dma(2), dma(2),
+            dma(2, 2), dma(2, 2), dma(2), dma(2), dma(2),
+            dma(4), dma(4), dma(4, 4), dma(4, 4), dma(2), dma(4, 2), dma(4, 2),
         ],
         compiler_params=pltpu.CompilerParams(collective_id=0, has_side_effects=True, vmem_limit_bytes=58 * MIB),
     )(query_nope[0], query_rope[0], grad_output[0], latent[0], key_rope[0].T, doc_lengths, kv_up)

time: 98.4 us -> 98.1 us (level)
  no operation moved by 1% of the time
where the time goes in v3:
time: 98.1 us; the launch traced here: 98 us
  Pallas kernels  97.4 us (99%)
    pallas_call x1, Pallas kernels, body(): pl.pallas_call(kernel, name='whole_rows', out_shape=(shape((BLOCK, HEADS...  95.1 us
    pallas_call x1, Pallas kernels, body(): pl.pallas_call(finish_kernel, name='finish_rows', out_shape=[shape(out.sh...  2.23 us

profile of v3, /device:TPU:1, one launch (start us, length us, event | category | flops | bytes accessed | tf_op | source)
XLA Modules:
  0.0 98.0 jit_solution(10550785822774873670)
XLA Ops:
  0.6 95.1 %whole_rows.1 = (bf16[128,2048]{1,0:T(8,128)(2,1)}, bf16[128,1024]{1,0:T(8,128)(2,1)}, bf16[128,512]{1,0:T(8,128)(2,1)}, bf16[64,128]{1,0:T(8,128)(2,1)}, f32[32,4096]{1,0:T(8,128)}) custom-call(bf16[128,2048]{1,0:T(8,128)(2,1)} %bitcast.13, bf16[128,1024]{1,0:T(8,128)(2,1)} %bitcast.15, bf16[128,2048]{1,0:T(8,128)(2,1)} %bitcast.14, ...), custom_call_target="tpu_custom_call" | custom-call | tf_op jit(solution)/shard_map/whole_rows/pallas_call | solution.py:703
  95.8 2.2 %finish_rows.1 = (bf16[128,2048]{1,0:T(8,128)(2,1)}, bf16[128,1024]{1,0:T(8,128)(2,1)}, bf16[128,512]{1,0:T(8,128)(2,1)}, bf16[64,128]{1,0:T(8,128)(2,1)}, f32[32,4096]{1,0:T(8,128)}) custom-call(bf16[128,2048]{1,0:T(8,128)(2,1)} %get-tuple-element.15.refs_0_, bf16[128,1024]{1,0:T(8,128)(2,1)} %get-tuple-element.16.refs_1_, ...), custom_call_target="tpu_custom_call" | custom-call | tf_op jit(solution)/shard_map/finish_rows/pallas_call | solution.py:764

commit v4 on v3

--- a/solution.py
+++ b/solution.py
@@ -439,15 +439,11 @@
         )
 
     def send_weights():
-        for n in range(GROUP):
-            wp[:, n * 256:(n + 1) * 256] = dot(latt[...], dkv[:, n * 256:(n + 1) * 256]).astype(BF16)
-
-            @pl.when(y != n)
-            def _():
-                slot = (n + 3 - y) % 4
-                remote(
-                    wp.at[:, pl.ds(n * 256, 256)], yin.at[slot], y_send.at[slot], y_recv.at[slot], device(zh, n, c, x, z)
-                ).start()
+        for d in (2, 1, 3, 0):
+            at = pl.ds(pl.multiple_of(((y + d) % 4) * 256, 256), 256)
+            wp[:, at] = dot(latt[...], dkv[:, at]).astype(BF16)
+            if d > 0:
+                y_copy(d).start()
 
     def s_copy(k, p):
         return remote(dkp.at[key_rows(p, k, 1 - c)], sin.at[p, k], s_send.at[k, p], s_recv.at[k, p], sib)

time: 98.1 us -> 98.1 us (level)
  no operation moved by 1% of the time
where the time goes in v4:
time: 98.1 us; the launch traced here: 98 us
  Pallas kernels  97.4 us (99%)
    pallas_call x1, Pallas kernels, body(): pl.pallas_call(kernel, name='whole_rows', out_shape=(shape((BLOCK, HEADS...  95.1 us
    pallas_call x1, Pallas kernels, body(): pl.pallas_call(finish_kernel, name='finish_rows', out_shape=[shape(out.sh...  2.23 us

profile of v4, /device:TPU:1, one launch (start us, length us, event | category | flops | bytes accessed | tf_op | source)
XLA Modules:
  0.0 98.0 jit_solution(15365351985631498170)
XLA Ops:
  0.6 95.1 %whole_rows.1 = (bf16[128,2048]{1,0:T(8,128)(2,1)}, bf16[128,1024]{1,0:T(8,128)(2,1)}, bf16[128,512]{1,0:T(8,128)(2,1)}, bf16[64,128]{1,0:T(8,128)(2,1)}, f32[32,4096]{1,0:T(8,128)}) custom-call(bf16[128,2048]{1,0:T(8,128)(2,1)} %bitcast.13, bf16[128,1024]{1,0:T(8,128)(2,1)} %bitcast.15, bf16[128,2048]{1,0:T(8,128)(2,1)} %bitcast.14, ...), custom_call_target="tpu_custom_call" | custom-call | tf_op jit(solution)/shard_map/whole_rows/pallas_call | solution.py:699
  95.8 2.2 %finish_rows.1 = (bf16[128,2048]{1,0:T(8,128)(2,1)}, bf16[128,1024]{1,0:T(8,128)(2,1)}, bf16[128,512]{1,0:T(8,128)(2,1)}, bf16[64,128]{1,0:T(8,128)(2,1)}, f32[32,4096]{1,0:T(8,128)}) custom-call(bf16[128,2048]{1,0:T(8,128)(2,1)} %get-tuple-element.15.refs_0_, bf16[128,1024]{1,0:T(8,128)(2,1)} %get-tuple-element.16.refs_1_, ...), custom_call_target="tpu_custom_call" | custom-call | tf_op jit(solution)/shard_map/finish_rows/pallas_call | solution.py:760
